TPU v7x, 32 devices: a whole 2x2x4 slice. The times are simulated.
32 devices in a mesh: replica: 8 (over y, x, core), fsdp: 4 (over z).
Axes of the slice: x: 2, y: 2, z: 4, core: 2. Of those that a mesh axis runs over, the one named last changes fastest.
Arguments:
- tokens: bfloat16 [4096, 4096], P(('replica', 'fsdp')), may hold values from -6 to 6
- out_grads: bfloat16 [4096, 14336], P(('replica', 'fsdp')), may hold values from -0.25 to 0.25
- block_ids: int32 [4], replicated, may hold values from 0 to 55, as said below
- left_basis: bfloat16 [8, 4, 1024, 1024], P('replica', 'fsdp'), may hold values from -0.1875 to 0.1875
- right_basis: bfloat16 [8, 4, 1024, 1024], P('replica', 'fsdp'), may hold values from -0.1875 to 0.1875
- first_moment: bfloat16 [8, 4, 1024, 1024], P('replica', 'fsdp'), may hold values from -3 to 3
- second_moment: bfloat16 [8, 4, 1024, 1024], P('replica', 'fsdp'), may hold values from 0.0099487305 to 1
- outer_params: float32 [512, 8192], P('fsdp'), may hold values from -6 to 6
- outer_momentum: float32 [512, 8192], P('fsdp'), may hold values from -3 to 3
- snapshot: bfloat16 [8, 512, 8192], P('replica', 'fsdp'), may hold values from -6 to 6
- local_params: bfloat16 [8, 512, 8192], P('replica', 'fsdp'), may hold values from -6 to 6
- due_rows: int32 [512], P('fsdp'), may hold values 0 or 1
Outputs:
- update: bfloat16 [8, 4, 1024, 1024], P('replica', 'fsdp')
- first_next: bfloat16 [8, 4, 1024, 1024], P('replica', 'fsdp')
- second_next: bfloat16 [8, 4, 1024, 1024], P('replica', 'fsdp')
- outer_next: float32 [512, 8192], P('fsdp')
- momentum_next: float32 [512, 8192], P('fsdp')
- local_next: bfloat16 [8, 512, 8192], P('replica', 'fsdp')
Inputs may be any that keep to these rules, and one draw needn't show every extreme that they name: `block_ids`: 4 different block numbers of the window; slot s belongs to fsdp index s.
All inputs are finite; a program needn't handle non-finite values. No bound on the sum of `due_rows` on one device may be relied on, other than what follows from the above.
Results may differ from a plain program's by a relative error of at most 0.022.
Values may be sent and summed in bfloat16 or wider, within the bound.
A program may use at most 192 MiB of HBM per device.

v0:
```python
import jax
import jax.numpy as jnp
from jax import lax
from jax.sharding import PartitionSpec as P

FW = 14336
BLOCK = 1024


def per_device(
    tokens,
    out_grads,
    block_ids,
    left_basis,
    right_basis,
    first_moment,
    second_moment,
    outer_params,
    outer_momentum,
    snapshot,
    local_params,
    due_rows,
):
    columns = FW // BLOCK
    owned = left_basis.shape[1]

    def block_cols(block):
        row_start = block // columns * BLOCK
        col_start = block % columns * BLOCK
        xcols = lax.dynamic_slice_in_dim(tokens, row_start, BLOCK, 1)
        dcols = lax.dynamic_slice_in_dim(out_grads, col_start, BLOCK, 1)
        return (xcols, dcols)

    def block_term(block):
        xcols, dcols = block_cols(block)
        return lax.dot_general(
            xcols, dcols, (((0,), (0,)), ((), ())), preferred_element_type=jnp.float32
        )

    summed = lax.psum_scatter(
        lax.map(block_term, block_ids)
        .reshape(lax.axis_size("fsdp") * (owned * BLOCK), BLOCK)
        .astype(jnp.bfloat16),
        "fsdp",
        scatter_dimension=0,
        tiled=True,
    )
    grad = summed.reshape(owned, BLOCK, BLOCK)
    lefts = left_basis[0]
    rights = right_basis[0]
    half = jnp.einsum("kij,kil->kjl", lefts, grad, preferred_element_type=jnp.float32).astype(
        jnp.bfloat16
    )
    rotated = jnp.einsum("kjl,klm->kjm", half, rights, preferred_element_type=jnp.float32)
    moment_one = 0.95 * first_moment[0].astype(jnp.float32) + 0.05 * rotated
    moment_two = 0.95 * second_moment[0].astype(jnp.float32) + 0.05 * rotated * rotated
    correct = 1.0 - 0.95**10
    direction = (moment_one / correct / (jnp.sqrt(moment_two / correct) + 1e-08)).astype(
        jnp.bfloat16
    )
    back = jnp.einsum("kij,kjl->kil", lefts, direction, preferred_element_type=jnp.float32).astype(
        jnp.bfloat16
    )
    update = jnp.einsum("kil,kml->kim", back, rights, preferred_element_type=jnp.float32).astype(
        jnp.bfloat16
    )
    snap = snapshot[0].astype(jnp.float32)
    pseudo = lax.psum((outer_params - snap).astype(jnp.bfloat16), "replica").astype(
        jnp.float32
    ) / lax.axis_size("replica")
    moment = 0.9 * outer_momentum + pseudo
    stepped = outer_params - 0.7 * (pseudo + 0.9 * moment)
    due = (due_rows == 1)[:, None]
    outer_next = jnp.where(due, stepped, outer_params)
    momentum_next = jnp.where(due, moment, outer_momentum)
    merged = (stepped + (local_params[0].astype(jnp.float32) - snap)).astype(jnp.bfloat16)
    local_next = jnp.where(due, merged, local_params[0])
    return (
        update[None],
        moment_one.astype(jnp.bfloat16)[None],
        moment_two.astype(jnp.bfloat16)[None],
        outer_next,
        momentum_next,
        local_next[None],
    )


def solution(mesh):
    return jax.shard_map(
        per_device,
        mesh=mesh,
        in_specs=(
            P(("replica", "fsdp"), None),
            P(("replica", "fsdp"), None),
            P(),
            P("replica", "fsdp", None, None),
            P("replica", "fsdp", None, None),
            P("replica", "fsdp", None, None),
            P("replica", "fsdp", None, None),
            P("fsdp", None),
            P("fsdp", None),
            P("replica", "fsdp", None),
            P("replica", "fsdp", None),
            P("fsdp"),
        ),
        out_specs=(
            P("replica", "fsdp", None, None),
            P("replica", "fsdp", None, None),
            P("replica", "fsdp", None, None),
            P("fsdp", None),
            P("fsdp", None),
            P("replica", "fsdp", None),
        ),
        check_vma=False,
    )
```

profile of v0, /device:TPU:0, one launch (start us, length us, event | category | flops | bytes accessed | tf_op | source)
XLA Modules:
  0.0 218.5 jit_solution(5506687398229980962)
XLA Ops:
  8.0 0.0 copy-start
  8.0 0.0 copy-start.4
  8.0 0.0 all-reduce.2.cloned.1.call-start
  8.1 4.7 %fusion.3 = bf16[128,8192]{1,0:T(8,128)(2,1)} fusion(f32[128,8192]{1,0:T(8,128)} %param.21, bf16[1,128,8192]{2,1,0:T(8,128)(2,1)} %param.23), kind=kLoop, calls=%fused_computation.8 | loop fusion | flops 3145728 | bytes 8388608 | tf_op jit(solution)/shard_map/convert_element_type | solution.py:68
  12.8 0.0 all-reduce.2.cloned.1.call-update
  12.8 0.0 reduce-scatter.2.cloned.1.call-start
  12.9 0.0 copy-done.4
  12.9 22.7 %while.12 = (s32[]{:T(128)}, bf16[4,1024,1024]{2,1,0:T(8,128)(2,1)}, s32[4]{0:T(128)S(1)}, bf16[128,4096]{1,0:T(8,128)(2,1)}, bf16[128,14336]{1,0:T(8,128)(2,1)}...) while((s32[]{:T(128)}, ...), condition=%wide.region_1.2_spmd, body=%wide.region_0.1_spmd.sunk | while | flops 268435488 | bytes 4718964 | solution.py:41
  12.9 0.6 dynamic_slice.28
  15.5 3.1 %bitcast_dynamic-update-slice_fusion.2 = bf16[4,1024,1024]{2,1,0:T(8,128)(2,1)} fusion(bf16[4,1024,1024]{2,1,0:T(8,128)(2,1)} %get-tuple-element.135, s32[]{:T(128)S(6)} %copy.21, bf16[128,14336]{1,0:T(8,128)(2,1)} %get-tuple-element.152, s32[]{:T(128)S(6)} %select_n.55, bf16[128,4096]{1,0:T(8,128)(2,1)} %get-tuple-element.151, s32[]{:T(128)S(6)} %select_n.57), kind=kOutput, calls=%fused_computation.clone.1 | convolution fusion | flops 268435456 | bytes 4718604 | tf_op jit(solution)/shard_map/while/body/eval_jaxpr/dot_general | solution.py:36
  18.6 0.6 dynamic_slice.28
  21.2 3.1 %bitcast_dynamic-update-slice_fusion.2 = bf16[4,1024,1024]{2,1,0:T(8,128)(2,1)} fusion(bf16[4,1024,1024]{2,1,0:T(8,128)(2,1)} %get-tuple-element.135, s32[]{:T(128)S(6)} %copy.21, bf16[128,14336]{1,0:T(8,128)(2,1)} %get-tuple-element.152, s32[]{:T(128)S(6)} %select_n.55, bf16[128,4096]{1,0:T(8,128)(2,1)} %get-tuple-element.151, s32[]{:T(128)S(6)} %select_n.57), kind=kOutput, calls=%fused_computation.clone.1 | convolution fusion | flops 268435456 | bytes 4718604 | tf_op jit(solution)/shard_map/while/body/eval_jaxpr/dot_general | solution.py:36
  24.2 0.6 dynamic_slice.28
  26.8 3.1 %bitcast_dynamic-update-slice_fusion.2 = bf16[4,1024,1024]{2,1,0:T(8,128)(2,1)} fusion(bf16[4,1024,1024]{2,1,0:T(8,128)(2,1)} %get-tuple-element.135, s32[]{:T(128)S(6)} %copy.21, bf16[128,14336]{1,0:T(8,128)(2,1)} %get-tuple-element.152, s32[]{:T(128)S(6)} %select_n.55, bf16[128,4096]{1,0:T(8,128)(2,1)} %get-tuple-element.151, s32[]{:T(128)S(6)} %select_n.57), kind=kOutput, calls=%fused_computation.clone.1 | convolution fusion | flops 268435456 | bytes 4718604 | tf_op jit(solution)/shard_map/while/body/eval_jaxpr/dot_general | solution.py:36
  29.9 0.6 dynamic_slice.28
  32.5 3.1 %bitcast_dynamic-update-slice_fusion.2 = bf16[4,1024,1024]{2,1,0:T(8,128)(2,1)} fusion(bf16[4,1024,1024]{2,1,0:T(8,128)(2,1)} %get-tuple-element.135, s32[]{:T(128)S(6)} %copy.21, bf16[128,14336]{1,0:T(8,128)(2,1)} %get-tuple-element.152, s32[]{:T(128)S(6)} %select_n.55, bf16[128,4096]{1,0:T(8,128)(2,1)} %get-tuple-element.151, s32[]{:T(128)S(6)} %select_n.57), kind=kOutput, calls=%fused_computation.clone.1 | convolution fusion | flops 268435456 | bytes 4718604 | tf_op jit(solution)/shard_map/while/body/eval_jaxpr/dot_general | solution.py:36
  35.6 0.0 copy-start.5
  35.6 0.0 reduce-scatter.2.cloned.1.call-update
  35.6 0.6 copy-done.5
  36.3 41.2 %all-reduce.2.cloned.1.call-done = bf16[128,8192]{1,0:T(8,128)(2,1)} async-done(((bf16[128,8192]{1,0:T(8,128)(2,1)}), bf16[128,8192]{1,0:T(8,128)(2,1)}) %all-reduce.2.cloned.1.call-update) | async-done | bytes 2097168 | tf_op jit(solution)/shard_map/psum | solution.py:68
  77.4 0.0 copy-start.1
  77.4 0.0 copy-start.2
  77.4 0.0 copy-start.3
  77.4 7.7 %fusion.13 = bf16[1,128,8192]{2,1,0:T(8,128)(2,1)} fusion(bf16[1,128,8192]{2,1,0:T(8,128)(2,1)} %param.23, bf16[1,128,8192]{2,1,0:T(8,128)(2,1)} %param.24, pred[128]{0:T(512)(128)(4,1)S(1)} %broadcast_compare_fusion, f32[128,8192]{1,0:T(8,128)} %param.21, f32[128,8192]{1,0:T(8,128)} %param.22, bf16[128,8192]{1,0:T(8,128)(2,1)} %all-reduce.2.cloned.1.call-done), kind=kLoop, calls=%fused_computation.22 | loop fusion | flops 14680064 | bytes 16777344 | tf_op jit(solution)/shard_map/broadcast_in_dim | solution.py:84
  85.2 0.0 copy-done.1
  85.2 0.9 copy-done.2
  86.1 0.6 copy-done.3
  86.6 4.8 %fusion.7 = (f32[128,8192]{1,0:T(8,128)}, f32[128,8192]{1,0:T(8,128)}) fusion(f32[128,8192]{1,0:T(8,128)S(1)} %copy-done.2, bf16[128,8192]{1,0:T(8,128)(2,1)S(1)} %copy-done.3, pred[128]{0:T(512)(128)(4,1)S(1)} %broadcast_compare_fusion, f32[128,8192]{1,0:T(8,128)S(1)} %copy-done.1), kind=kLoop, calls=%fused_computation.14 | loop fusion | flops 10485760 | bytes 18874496 | tf_op jit(solution)/shard_map/jit(_where)/select_n | solution.py:75
  91.4 91.5 %reduce-scatter.2.cloned.1.call-done = bf16[1024,1024]{1,0:T(8,128)(2,1)} async-done(((bf16[4096,1024]{1,0:T(8,128)(2,1)}), bf16[1024,1024]{1,0:T(8,128)(2,1)}) %reduce-scatter.2.cloned.1.call-update) | async-done | bytes 2097168 | tf_op jit(solution)/shard_map/reduce_scatter | solution.py:40
  182.9 0.0 copy-done
  182.9 8.7 %fusion.16 = f32[1024,1024]{1,0:T(8,128)} fusion(bf16[1,1,1024,1024]{3,2,1,0:T(8,128)(2,1)S(1)} %copy-done, bf16[1024,1024]{1,0:T(8,128)(2,1)} %reduce-scatter.2.cloned.1.call-done, bf16[1,1,1024,1024]{3,2,1,0:T(8,128)(2,1)} %param.17), kind=kOutput, calls=%fused_computation.25 | convolution fusion | flops 4296015872 | bytes 10485760 | tf_op jit(solution)/shard_map/kjl,klm->kjm/dot_general | solution.py:54
  191.7 12.5 %convert_bitcast_fusion = bf16[1,1,1024,1024]{3,2,1,0:T(8,128)(2,1)} fusion(bf16[1,1,1024,1024]{3,2,1,0:T(8,128)(2,1)S(1)} %copy-done, bf16[1,1,1024,1024]{3,2,1,0:T(8,128)(2,1)} %param.17, f32[1024,1024]{1,0:T(8,128)} %fusion.16, bf16[1,1,1024,1024]{3,2,1,0:T(8,128)(2,1)} %param.19, bf16[1,1,1024,1024]{3,2,1,0:T(8,128)(2,1)} %param.20), kind=kOutput, calls=%fused_computation.31 | convolution fusion | flops 4310695936 | bytes 14680064 | tf_op jit(solution)/shard_map/kil,kml->kim/dot_general | solution.py:64
  204.2 6.9 %fusion.11 = (bf16[1,1,1024,1024]{3,2,1,0:T(8,128)(2,1)}, bf16[1,1,1024,1024]{3,2,1,0:T(8,128)(2,1)}) fusion(f32[1024,1024]{1,0:T(8,128)} %fusion.16, bf16[1,1,1024,1024]{3,2,1,0:T(8,128)(2,1)} %param.20, bf16[1,1,1024,1024]{3,2,1,0:T(8,128)(2,1)} %param.19), kind=kLoop, calls=%fused_computation.20 | loop fusion | flops 10485760 | bytes 12582912 | tf_op jit(solution)/shard_map/broadcast_in_dim | solution.py:81
  (2 shorter events, 0.0 us)
Async XLA Ops:
  8.0 174.9 %copy-start = (bf16[1,1,1024,1024]{3,2,1,0:T(8,128)(2,1)S(1)}, bf16[1,1,1024,1024]{3,2,1,0:T(8,128)(2,1)}, u32[]{:S(2)}) copy-start(bf16[1,1,1024,1024]{3,2,1,0:T(8,128)(2,1)} %param.18) | copy-start | bytes 6291460
  8.0 4.9 %copy-start.4 = (s32[4]{0:T(128)S(1)}, s32[4]{0:T(128)}, u32[]{:S(2)}) copy-start(s32[4]{0:T(128)} %param.16) | copy-start | bytes 52
  8.0 69.4 %all-reduce.2.cloned.1.call-start = ((), (), s32[]{:S(2)}) async-start(), calls=%async_computation.2 | async-start | bytes 4194304 | tf_op jit(solution)/shard_map/psum | solution.py:68
  12.8 170.1 %reduce-scatter.2.cloned.1.call-start = ((), (), s32[]{:S(2)}) async-start(), calls=%async_computation.1 | async-start | bytes 10485760 | tf_op jit(solution)/shard_map/reduce_scatter | solution.py:40
  35.6 0.7 copy-start.5
  77.4 7.7 %copy-start.1 = (f32[128,8192]{1,0:T(8,128)S(1)}, f32[128,8192]{1,0:T(8,128)}, u32[]{:S(2)}) copy-start(f32[128,8192]{1,0:T(8,128)} %param.21) | copy-start | bytes 12582916
  77.4 8.6 %copy-start.2 = (f32[128,8192]{1,0:T(8,128)S(1)}, f32[128,8192]{1,0:T(8,128)}, u32[]{:S(2)}) copy-start(f32[128,8192]{1,0:T(8,128)} %param.22) | copy-start | bytes 12582916
  77.4 9.2 %copy-start.3 = (bf16[128,8192]{1,0:T(8,128)(2,1)S(1)}, bf16[128,8192]{1,0:T(8,128)(2,1)}, u32[]{:S(2)}) copy-start(bf16[128,8192]{1,0:T(8,128)(2,1)} %all-reduce.2.cloned.1.call-done) | copy-start | bytes 6291460
Sparse Core Ops, SparseCore 0:
  12.9 64.4 all-reduce.1
Sparse Core Ops, SparseCore 1:
  35.7 147.1 reduce-scatter.1
where the time goes:
time: 219 us
  waiting for transfers between devices  133 us (61%)
  matrix products  33.7 us (15%)
  other arithmetic  24.2 us (11%)
  between operations  15.5 us (7%)
  loops' own time  7.96 us (4%)
  local copies, waits for them, and re-layouts  4.47 us (2%)
    reduce_scatter x1, waiting for transfers between devices, per_device(): lax.psum_scatter(lax.map(block_term, block_ids).reshape(lax.axis_size('fs...  91.5 us
    psum x1, waiting for transfers between devices, per_device(): lax.psum((outer_params - snap).astype(jnp.bfloat16), 'replica')  41.2 us
    dot_general x1, matrix products, per_device(): jnp.einsum('kil,kml->kim', back, rights, preferred_element_type=jnp.float32)  12.5 us
    dot_general x4, matrix products, block_term(): lax.dot_general(xcols, dcols, (((0,), (0,)), ((), ())), preferred_element...  12.4 us
    dot_general x1, matrix products, per_device(): jnp.einsum('kjl,klm->kjm', half, rights, preferred_element_type=jnp.float32)  8.75 us
    another operation x1, loops' own time, per_device(): lax.map(block_term, block_ids)  7.96 us
    broadcast_in_dim x1, other arithmetic, per_device(): local_next[None]  7.72 us
    broadcast_in_dim x1, other arithmetic, per_device(): moment_two.astype(jnp.bfloat16)[None]  6.92 us
  transfers between devices with their start and end apart: 2, of which 2 were waited for; matrix products, arithmetic and copies ran while one was open for 12% of the time, Pallas kernels for 0%

commit v1 on v0

v1 whole, which is shorter than its diff:
```python
import jax
import jax.numpy as jnp
from jax import lax
from jax.sharding import PartitionSpec as P


def per_device(
    tokens,
    out_grads,
    block_ids,
    left_basis,
    right_basis,
    first_moment,
    second_moment,
    outer_params,
    outer_momentum,
    snapshot,
    local_params,
    due_rows,
):
    width = left_basis.shape[-1]
    columns = out_grads.shape[1] // width
    n = lax.axis_size("fsdp")
    me = lax.axis_index("fsdp")
    left = left_basis[0, 0]
    right = right_basis[0, 0]

    def block_cols(slot):
        block = block_ids[slot]
        xcols = lax.dynamic_slice_in_dim(tokens, block // columns * width, width, 1)
        dcols = lax.dynamic_slice_in_dim(out_grads, block % columns * width, width, 1)
        return jnp.stack([xcols, dcols])

    arrived = [block_cols(me)]
    for shift in range(1, n):
        arrived.append(
            lax.ppermute(
                block_cols((me + shift) % n),
                "fsdp",
                [(i, (i + shift) % n) for i in range(n)],
            )
        )
    snap_sum = lax.psum(snapshot[0], "replica").astype(jnp.float32)

    xl = [
        jnp.dot(part[0], left, preferred_element_type=jnp.float32).astype(jnp.bfloat16)
        for part in arrived
    ]
    dr = [
        jnp.dot(part[1], right, preferred_element_type=jnp.float32).astype(jnp.bfloat16)
        for part in arrived
    ]
    rotated = lax.dot_general(
        jnp.concatenate(xl),
        jnp.concatenate(dr),
        (((0,), (0,)), ((), ())),
        preferred_element_type=jnp.float32,
    )
    moment_one = 0.95 * first_moment[0, 0].astype(jnp.float32) + 0.05 * rotated
    moment_two = 0.95 * second_moment[0, 0].astype(jnp.float32) + 0.05 * rotated * rotated
    correct = 1.0 - 0.95**10
    direction = (moment_one / correct / (jnp.sqrt(moment_two / correct) + 1e-08)).astype(
        jnp.bfloat16
    )
    back = jnp.dot(left, direction, preferred_element_type=jnp.float32).astype(jnp.bfloat16)
    update = lax.dot_general(
        back, right, (((1,), (1,)), ((), ())), preferred_element_type=jnp.float32
    ).astype(jnp.bfloat16)

    snap = snapshot[0].astype(jnp.float32)
    pseudo = outer_params - snap_sum / lax.axis_size("replica")
    moment = 0.9 * outer_momentum + pseudo
    stepped = outer_params - 0.7 * (pseudo + 0.9 * moment)
    due = (due_rows == 1)[:, None]
    outer_next = jnp.where(due, stepped, outer_params)
    momentum_next = jnp.where(due, moment, outer_momentum)
    merged = (stepped + (local_params[0].astype(jnp.float32) - snap)).astype(jnp.bfloat16)
    local_next = jnp.where(due, merged, local_params[0])
    return (
        update[None, None],
        moment_one.astype(jnp.bfloat16)[None, None],
        moment_two.astype(jnp.bfloat16)[None, None],
        outer_next,
        momentum_next,
        local_next[None],
    )


def solution(mesh):
    return jax.shard_map(
        per_device,
        mesh=mesh,
        in_specs=(
            P(("replica", "fsdp"), None),
            P(("replica", "fsdp"), None),
            P(),
            P("replica", "fsdp", None, None),
            P("replica", "fsdp", None, None),
            P("replica", "fsdp", None, None),
            P("replica", "fsdp", None, None),
            P("fsdp", None),
            P("fsdp", None),
            P("replica", "fsdp", None),
            P("replica", "fsdp", None),
            P("fsdp"),
        ),
        out_specs=(
            P("replica", "fsdp", None, None),
            P("replica", "fsdp", None, None),
            P("replica", "fsdp", None, None),
            P("fsdp", None),
            P("fsdp", None),
            P("replica", "fsdp", None),
        ),
        check_vma=False,
    )
```

time: 219 us -> 110 us (0.50)
  the two profiles are of different devices: /device:TPU:0 before, /device:TPU:11 now
where the time goes in v1:
time: 110 us; the launch traced here: 109 us
  waiting for transfers between devices  34.1 us (31%)
  matrix products  23.8 us (22%)
  between operations  22.2 us (20%)
  other arithmetic  16.9 us (15%)
  local copies, waits for them, and re-layouts  8.29 us (8%)
  starting transfers between devices  3.81 us (3%)
    ppermute x3, waiting for transfers between devices, per_device(): lax.ppermute(block_cols((me + shift) % n), 'fsdp', [(i, (i + shift) % n)...  34.1 us
    dot_general x1, matrix products, per_device(): lax.dot_general(back, right, (((1,), (1,)), ((), ())), preferred_element_...  12.7 us
    select_n x1, other arithmetic, per_device(): momentum_next = jnp.where(due, moment, outer_momentum)  7.88 us
    dot_general x4, matrix products, per_device(): jnp.dot(part[0], left, preferred_element_type=jnp.float32)  6.01 us
    unnamed x22, local copies, waits for them, and re-layouts  5.36 us
    dot_general x4, matrix products, per_device(): jnp.dot(part[1], right, preferred_element_type=jnp.float32)  3.85 us
    ppermute x3, starting transfers between devices, per_device(): lax.ppermute(block_cols((me + shift) % n), 'fsdp', [(i, (i + shift) % n)...  3.77 us
    broadcast_in_dim x1, other arithmetic, per_device(): moment_two.astype(jnp.bfloat16)[None, None]  3.49 us
  transfers between devices with their start and end apart: 4, of which 3 were waited for; matrix products, arithmetic and copies ran while one was open for 27% of the time, Pallas kernels for 0%

profile of v1, /device:TPU:11, one launch (start us, length us, event | category | flops | bytes accessed | tf_op | source)
XLA Modules:
  0.0 109.2 jit_solution(8893538254582556164)
XLA Ops:
  7.2 0.0 copy-start
  7.2 0.0 all-reduce.2.cloned.1.call-start
  7.3 1.4 %fusion.89 = (s32[1]{0:T(128)}, s32[1]{0:T(128)}, s32[1]{0:T(128)}, s32[1]{0:T(128)}) fusion(s32[4]{0:T(128)} %param.14, s32[]{:T(128)S(6)} %select_n.91, s32[]{:T(128)S(6)} %select_n.95, s32[]{:T(128)S(6)} %select_n.107, s32[]{:T(128)S(6)} %select_n.101), kind=kLoop, calls=%fused_computation.86 | loop fusion | bytes 48 | tf_op jit(solution)/shard_map/dynamic_slice | solution.py:29
  14.6 1.5 %dynamic-slice_bitcast_fusion.4 = (bf16[1,128,1024]{2,1,0:T(8,128)(2,1)S(1)}, bf16[1,128,1024]{2,1,0:T(8,128)(2,1)S(1)}, bf16[1,128,1024]{2,1,0:T(8,128)(2,1)S(1...) fusion(bf16[128,14336]{1,0:T(8,128)(2,1)} %param.13, ...), kind=kLoop, calls=%fused_computation.75 | loop fusion | bytes 3145752 | tf_op jit(solution)/shard_map/stack | solution.py:32
  16.1 0.8 pad_maximum_fusion
  17.0 0.0 copy-start.10
  17.0 1.3 %collective-permute-start = (bf16[2,128,1024]{2,1,0:T(8,128)(2,1)}, bf16[2,128,1024]{2,1,0:T(8,128)(2,1)S(1)}, u32[]{:S(2)}, u32[]{:S(2)}) collective-permute-start(bf16[2,128,1024]{2,1,0:T(8,128)(2,1)} %pad_maximum_fusion), channel_id=1, source_target_pairs={{0,1},{1,2},{2,3},{3,0},{4,5},{5,6},{6,7},{7,4},{8,9},{9,10},{10,1... | collective-permute-start | bytes 1572872 | tf_op jit(solution)/shard_map/ppermute | solution.py:37
  18.3 0.8 pad_maximum_fusion.1
  19.1 1.0 collective-permute-start.1
  20.1 0.8 pad_maximum_fusion.2
  21.0 1.5 %collective-permute-start.2 = (bf16[2,128,1024]{2,1,0:T(8,128)(2,1)}, bf16[2,128,1024]{2,1,0:T(8,128)(2,1)}, u32[]{:S(2)}, u32[]{:S(2)}) collective-permute-start(bf16[2,128,1024]{2,1,0:T(8,128)(2,1)} %pad_maximum_fusion.2), channel_id=1, source_target_pairs={{0,3},{1,0},{2,1},{3,2},{4,7},{5,4},{6,5},{7,6},{8,11},{9,8},{10,9... | collective-permute-start | bytes 1572872 | tf_op jit(solution)/shard_map/ppermute | solution.py:37
  22.4 0.0 all-reduce.2.cloned.1.call-update
  24.4 2.1 %fusion.37 = bf16[128,1024]{1,0:T(8,128)(2,1)S(1)} fusion(bf16[1,1,1024,1024]{3,2,1,0:T(8,128)(2,1)} %param.15, bf16[128,4096]{1,0:T(8,128)(2,1)} %param.12, s32[]{:T(128)S(6)} %select_n.93), kind=kOutput, calls=%fused_computation.38 | convolution fusion | flops 268566528 | bytes 2621444 | tf_op jit(solution)/shard_map/dot_general | solution.py:46
  26.6 0.0 copy-done.10
  26.6 0.0 copy-done
  26.6 0.0 copy-start.1
  26.6 1.6 %fusion.49 = bf16[128,1024]{1,0:T(8,128)(2,1)S(1)} fusion(bf16[1,1,1024,1024]{3,2,1,0:T(8,128)(2,1)S(1)} %copy-done, bf16[128,14336]{1,0:T(8,128)(2,1)} %param.13, s32[]{:T(128)S(6)} %select_n.113), kind=kOutput, calls=%fused_computation.42 | convolution fusion | flops 268566528 | bytes 2621444 | tf_op jit(solution)/shard_map/dot_general | solution.py:50
  28.2 1.9 %collective-permute-done = bf16[2,128,1024]{2,1,0:T(8,128)(2,1)S(1)} collective-permute-done((bf16[2,128,1024]{2,1,0:T(8,128)(2,1)}, bf16[2,128,1024]{2,1,0:T(8,128)(2,1)S(1)}, u32[]{:S(2)}, u32[]{:S(2)}) %collective-permute-start) | collective-permute-done | bytes 524320 | tf_op jit(solution)/shard_map/ppermute | solution.py:37
  30.1 2.0 %fusion.40 = bf16[128,1024]{1,0:T(8,128)(2,1)S(1)} fusion(bf16[1,1,1024,1024]{3,2,1,0:T(8,128)(2,1)} %param.15, bf16[2,128,1024]{2,1,0:T(8,128)(2,1)S(1)} %collective-permute-done), kind=kOutput, calls=%fused_computation.39 | convolution fusion | flops 268566528 | bytes 2621440 | tf_op jit(solution)/shard_map/dot_general | solution.py:46
  32.1 0.4 fusion.52
  32.6 30.3 %collective-permute-done.1 = bf16[2,128,1024]{2,1,0:T(8,128)(2,1)S(1)} collective-permute-done((bf16[2,128,1024]{2,1,0:T(8,128)(2,1)}, bf16[2,128,1024]{2,1,0:T(8,128)(2,1)S(1)}, u32[]{:S(2)}, u32[]{:S(2)}) %collective-permute-start.1) | collective-permute-done | bytes 524320 | tf_op jit(solution)/shard_map/ppermute | solution.py:37
  62.9 0.0 copy-done.1
  62.9 0.4 fusion.43
  63.4 0.5 fusion.55
  63.8 1.9 %collective-permute-done.2 = bf16[2,128,1024]{2,1,0:T(8,128)(2,1)} collective-permute-done((bf16[2,128,1024]{2,1,0:T(8,128)(2,1)}, bf16[2,128,1024]{2,1,0:T(8,128)(2,1)}, u32[]{:S(2)}, u32[]{:S(2)}) %collective-permute-start.2) | collective-permute-done | bytes 524320 | tf_op jit(solution)/shard_map/ppermute | solution.py:37
  65.7 1.4 %fusion.46 = bf16[128,1024]{1,0:T(8,128)(2,1)S(1)} fusion(bf16[1,1,1024,1024]{3,2,1,0:T(8,128)(2,1)S(1)} %copy-done.1, bf16[2,128,1024]{2,1,0:T(8,128)(2,1)} %collective-permute-done.2), kind=kOutput, calls=%fused_computation.41 | convolution fusion | flops 268566528 | bytes 2621440 | tf_op jit(solution)/shard_map/dot_general | solution.py:46
  67.1 1.4 %fusion.58 = bf16[128,1024]{1,0:T(8,128)(2,1)S(1)} fusion(bf16[1,1,1024,1024]{3,2,1,0:T(8,128)(2,1)S(1)} %copy-done, bf16[2,128,1024]{2,1,0:T(8,128)(2,1)} %collective-permute-done.2), kind=kOutput, calls=%fused_computation.45 | convolution fusion | flops 268566528 | bytes 2621440 | tf_op jit(solution)/shard_map/dot_general | solution.py:50
  68.5 0.0 copy-start.8
  68.6 0.0 copy-start.9
  68.6 1.3 %fusion.61 = f32[1024,1024]{1,0:T(8,128)S(1)} fusion(bf16[128,1024]{1,0:T(8,128)(2,1)S(1)} %fusion.46, bf16[128,1024]{1,0:T(8,128)(2,1)S(1)} %fusion.43, bf16[128,1024]{1,0:T(8,128)(2,1)S(1)} %fusion.40, bf16[128,1024]{1,0:T(8,128)(2,1)S(1)} %fusion.37, bf16[128,1024]{1,0:T(8,128)(2,1)S(1)} %fusion.58, bf16[128,1024]{1,0:T(8,128)(2,1)S(1)} %fusion.55, ...), kind=kOutput, calls=%fused_computation.46 | convolution fusion | flops 1082130432 | bytes 6291456 | tf_op jit(solution)/shard_map/dot_general | solution.py:53
  69.9 0.0 copy-start.6
  69.9 2.0 %copy-done.6 = f32[1024,1024]{1,0:T(8,128)} copy-done((f32[1024,1024]{1,0:T(8,128)}, f32[1024,1024]{1,0:T(8,128)S(1)}, u32[]{:S(2)}) %copy-start.6) | copy-done | bytes 4194328
  71.9 0.0 copy-done.8
  71.9 0.0 copy-done.9
  71.9 3.5 %fusion.5 = (bf16[1,1,1024,1024]{3,2,1,0:T(8,128)(2,1)}, bf16[1,1,1024,1024]{3,2,1,0:T(8,128)(2,1)}) fusion(f32[1024,1024]{1,0:T(8,128)S(1)} %fusion.61, bf16[1,1,1024,1024]{3,2,1,0:T(8,128)(2,1)S(1)} %copy-done.9, bf16[1,1,1024,1024]{3,2,1,0:T(8,128)(2,1)S(1)} %copy-done.8), kind=kLoop, calls=%fused_computation.12 | loop fusion | flops 10485760 | bytes 12582912 | tf_op jit(solution)/shard_map/broadcast_in_dim | solution.py:82
  75.4 12.7 %convert_bitcast_fusion = bf16[1,1,1024,1024]{3,2,1,0:T(8,128)(2,1)} fusion(bf16[1,1,1024,1024]{3,2,1,0:T(8,128)(2,1)S(1)} %copy-done, bf16[1,1,1024,1024]{3,2,1,0:T(8,128)(2,1)} %param.15, f32[1024,1024]{1,0:T(8,128)} %copy-done.6, bf16[1,1,1024,1024]{3,2,1,0:T(8,128)(2,1)} %param.17, bf16[1,1,1024,1024]{3,2,1,0:T(8,128)(2,1)} %param.18), kind=kOutput, calls=%fused_computation.35 | convolution fusion | flops 4310695936 | bytes 14680064 | tf_op jit(solution)/shard_map/dot_general | solution.py:66
  88.1 0.0 all-reduce.2.cloned.1.call-done
  88.1 0.0 copy-start.2
  88.1 0.0 copy-start.3
  88.1 0.0 copy-start.5
  88.1 0.0 copy-start.7
  88.1 7.9 %fusion.1 = (f32[128,8192]{1,0:T(8,128)}, f32[128,8192]{1,0:T(8,128)}) fusion(f32[128,8192]{1,0:T(8,128)} %param.20, f32[128,8192]{1,0:T(8,128)} %param.19, bf16[128,8192]{1,0:T(8,128)(2,1)} %all-reduce.2.cloned.1.call-done, pred[128]{0:T(512)(128)(4,1)S(1)} %broadcast_compare_fusion), kind=kLoop, calls=%fused_computation.6 | loop fusion | flops 11534336 | bytes 18874496 | tf_op jit(solution)/shard_map/jit(_where)/select_n | solution.py:76
  96.0 0.0 copy-done.2
  96.0 1.5 %copy-done.3 = f32[128,8192]{1,0:T(8,128)S(1)} copy-done((f32[128,8192]{1,0:T(8,128)S(1)}, f32[128,8192]{1,0:T(8,128)}, u32[]{:S(2)}) %copy-start.3) | copy-done | bytes 4194328
  97.5 0.6 copy-done.4
  98.1 0.6 copy-done.5
  98.7 0.6 copy-done.7
  99.3 3.0 %fusion.7 = bf16[1,128,8192]{2,1,0:T(8,128)(2,1)} fusion(bf16[1,128,8192]{2,1,0:T(8,128)(2,1)S(1)} %copy-done.7, pred[128]{0:T(512)(128)(4,1)S(1)} %broadcast_compare_fusion, f32[128,8192]{1,0:T(8,128)S(1)} %copy-done.3, f32[128,8192]{1,0:T(8,128)S(1)} %copy-done.2, bf16[128,8192]{1,0:T(8,128)(2,1)S(1)} %copy-done.5, bf16[1,128,8192]{2,1,0:T(8,128)(2,1)S(1)} %copy-done.4), kind=kLoop, calls=%fused_computation.14 | loop fusion | flops 15728640 | bytes 16777344 | tf_op jit(solution)/shard_map/broadcast_in_dim | solution.py:85
  (2 shorter events, 0.0 us)
Async XLA Ops:
  7.2 19.5 %copy-start = (bf16[1,1,1024,1024]{3,2,1,0:T(8,128)(2,1)S(1)}, bf16[1,1,1024,1024]{3,2,1,0:T(8,128)(2,1)}, u32[]{:S(2)}) copy-start(bf16[1,1,1024,1024]{3,2,1,0:T(8,128)(2,1)} %param.16) | copy-start | bytes 6291460
  7.2 80.9 %all-reduce.2.cloned.1.call-start = ((), (), s32[]{:S(2)}) async-start(), calls=%async_computation | async-start | bytes 4194304 | tf_op jit(solution)/shard_map/psum | solution.py:43
  17.0 9.6 %copy-start.10 = (s32[128]{0:T(128)S(1)}, s32[128]{0:T(128)}, u32[]{:S(2)}) copy-start(s32[128]{0:T(128)} %param.23) | copy-start | bytes 1540
  17.0 13.1 %collective-permute-start = (bf16[2,128,1024]{2,1,0:T(8,128)(2,1)}, bf16[2,128,1024]{2,1,0:T(8,128)(2,1)S(1)}, u32[]{:S(2)}, u32[]{:S(2)}) collective-permute-start(bf16[2,128,1024]{2,1,0:T(8,128)(2,1)} %pad_maximum_fusion), channel_id=1, source_target_pairs={{0,1},{1,2},{2,3},{3,0},{4,5},{5,6},{6,7},{7,4},{8,9},{9,10},{10,1... | collective-permute-start | bytes 1572872 | tf_op jit(solution)/shard_map/ppermute | solution.py:37
  19.1 43.8 %collective-permute-start.1 = (bf16[2,128,1024]{2,1,0:T(8,128)(2,1)}, bf16[2,128,1024]{2,1,0:T(8,128)(2,1)S(1)}, u32[]{:S(2)}, u32[]{:S(2)}) collective-permute-start(bf16[2,128,1024]{2,1,0:T(8,128)(2,1)} %pad_maximum_fusion.1), channel_id=1, source_target_pairs={{0,2},{1,3},{2,0},{3,1},{4,6},{5,7},{6,4},{7,5},{8,10},{9,11},{10,... | collective-permute-start | bytes 1572872 | tf_op jit(solution)/shard_map/ppermute | solution.py:37
  21.0 44.8 %collective-permute-start.2 = (bf16[2,128,1024]{2,1,0:T(8,128)(2,1)}, bf16[2,128,1024]{2,1,0:T(8,128)(2,1)}, u32[]{:S(2)}, u32[]{:S(2)}) collective-permute-start(bf16[2,128,1024]{2,1,0:T(8,128)(2,1)} %pad_maximum_fusion.2), channel_id=1, source_target_pairs={{0,3},{1,0},{2,1},{3,2},{4,7},{5,4},{6,5},{7,6},{8,11},{9,8},{10,9... | collective-permute-start | bytes 1572872 | tf_op jit(solution)/shard_map/ppermute | solution.py:37
  26.6 36.3 %copy-start.1 = (bf16[1,1,1024,1024]{3,2,1,0:T(8,128)(2,1)S(1)}, bf16[1,1,1024,1024]{3,2,1,0:T(8,128)(2,1)}, u32[]{:S(2)}) copy-start(bf16[1,1,1024,1024]{3,2,1,0:T(8,128)(2,1)} %param.15) | copy-start | bytes 6291460
  68.5 3.3 %copy-start.8 = (bf16[1,1,1024,1024]{3,2,1,0:T(8,128)(2,1)S(1)}, bf16[1,1,1024,1024]{3,2,1,0:T(8,128)(2,1)}, u32[]{:S(2)}) copy-start(bf16[1,1,1024,1024]{3,2,1,0:T(8,128)(2,1)} %param.17) | copy-start | bytes 6291460
  68.6 3.3 %copy-start.9 = (bf16[1,1,1024,1024]{3,2,1,0:T(8,128)(2,1)S(1)}, bf16[1,1,1024,1024]{3,2,1,0:T(8,128)(2,1)}, u32[]{:S(2)}) copy-start(bf16[1,1,1024,1024]{3,2,1,0:T(8,128)(2,1)} %param.18) | copy-start | bytes 6291460
  69.9 2.0 %copy-start.6 = (f32[1024,1024]{1,0:T(8,128)}, f32[1024,1024]{1,0:T(8,128)S(1)}, u32[]{:S(2)}) copy-start(f32[1024,1024]{1,0:T(8,128)S(1)} %fusion.61) | copy-start | bytes 12582916
  88.1 7.9 %copy-start.2 = (f32[128,8192]{1,0:T(8,128)S(1)}, f32[128,8192]{1,0:T(8,128)}, u32[]{:S(2)}) copy-start(f32[128,8192]{1,0:T(8,128)} %param.20) | copy-start | bytes 12582916
  88.1 9.4 %copy-start.3 = (f32[128,8192]{1,0:T(8,128)S(1)}, f32[128,8192]{1,0:T(8,128)}, u32[]{:S(2)}) copy-start(f32[128,8192]{1,0:T(8,128)} %param.19) | copy-start | bytes 12582916
  88.1 10.0 %copy-start.4 = (bf16[1,128,8192]{2,1,0:T(8,128)(2,1)S(1)}, bf16[1,128,8192]{2,1,0:T(8,128)(2,1)}, u32[]{:S(2)}) copy-start(bf16[1,128,8192]{2,1,0:T(8,128)(2,1)} %param.21) | copy-start | bytes 6291460
  88.1 10.6 %copy-start.5 = (bf16[128,8192]{1,0:T(8,128)(2,1)S(1)}, bf16[128,8192]{1,0:T(8,128)(2,1)}, u32[]{:S(2)}) copy-start(bf16[128,8192]{1,0:T(8,128)(2,1)} %all-reduce.2.cloned.1.call-done) | copy-start | bytes 6291460
  88.1 11.2 %copy-start.7 = (bf16[1,128,8192]{2,1,0:T(8,128)(2,1)S(1)}, bf16[1,128,8192]{2,1,0:T(8,128)(2,1)}, u32[]{:S(2)}) copy-start(bf16[1,128,8192]{2,1,0:T(8,128)(2,1)} %param.22) | copy-start | bytes 6291460
Sparse Core Ops, SparseCore 0:
  22.6 59.7 all-reduce.1

commit v2 on v1

v2 whole, which is shorter than its diff:
```python
import functools

import jax
import jax.numpy as jnp
from jax import lax
from jax.experimental import pallas as pl
from jax.experimental.pallas import tpu as pltpu
from jax.sharding import PartitionSpec as P

MIB = 1 << 20
CORES = 2
CORRECT = 1.0 - 0.95**10


def any_spec():
    return pl.BlockSpec(memory_space=pl.ANY)


def vmem_spec():
    return pl.BlockSpec(memory_space=pltpu.VMEM)


def gather_kernel(n, width, columns, order, ids, tokens, out_grads, *refs):
    outs, sems = refs[:n], refs[n]
    me = lax.axis_index("fsdp")
    copies = []
    for k, shift in enumerate(order):
        block = ids[lax.rem(me + shift, n)]
        row = pl.multiple_of(block // columns * width, width)
        col = pl.multiple_of(lax.rem(block, columns) * width, width)
        copies.append(
            pltpu.make_async_copy(tokens.at[:, pl.ds(row, width)], outs[k].at[0], sems.at[0, k])
        )
        copies.append(
            pltpu.make_async_copy(out_grads.at[:, pl.ds(col, width)], outs[k].at[1], sems.at[1, k])
        )
    for copy in copies:
        copy.start()
    for copy in copies:
        copy.wait()


def gather(tokens, out_grads, block_ids, width, n, order):
    rows = tokens.shape[0]
    return pl.pallas_call(
        functools.partial(gather_kernel, n, width, out_grads.shape[1] // width, order),
        out_shape=[jax.ShapeDtypeStruct((2, rows, width), tokens.dtype)] * n,
        in_specs=[pl.BlockSpec(memory_space=pltpu.SMEM), any_spec(), any_spec()],
        out_specs=[any_spec()] * n,
        scratch_shapes=[pltpu.SemaphoreType.DMA((2, n))],
        compiler_params=pltpu.CompilerParams(vmem_limit_bytes=4 * MIB),
        cost_estimate=pl.CostEstimate(flops=0, bytes_accessed=16 * n * rows * width, transcendentals=0),
        name="gather_slots",
    )(block_ids, tokens, out_grads)


def sum_kernel(
    chips, own, out, sib, part, inbox, s1, r1, s2, r2, s3, r3, s4, r4
):
    me = lax.axis_index("replica")
    chip, core = me // CORES, lax.rem(me, CORES)
    half, wide = own.shape[0] // CORES, own.shape[1] // chips
    other = 1 - core
    sibling = {"replica": chip * CORES + other}

    def peer(k):
        return lax.rem(chip + k, chips)

    def rows(c):
        return pl.ds(pl.multiple_of(c * half, half), half)

    def cols(c):
        return pl.ds(pl.multiple_of(c * wide, wide), wide)

    def to(k):
        return {"replica": peer(k) * CORES + core}

    barrier = pltpu.get_barrier_semaphore()
    pl.semaphore_signal(barrier, inc=1, device_id=sibling, device_id_type=pl.DeviceIdType.MESH)
    for k in range(1, chips):
        pl.semaphore_signal(barrier, inc=1, device_id=to(k), device_id_type=pl.DeviceIdType.MESH)
    pl.semaphore_wait(barrier, chips)

    turns = list(range(1, chips)) + [0]
    remote = functools.partial(
        pltpu.make_async_remote_copy, device_id_type=pl.DeviceIdType.MESH
    )
    first = {
        k: remote(own.at[rows(other), cols(peer(k))], sib.at[k], s1.at[k], r1.at[k], device_id=sibling)
        for k in turns
    }
    for k in turns:
        first[k].start()
    second = {}
    for k in turns:
        first[k].wait_recv()
        pair = own[rows(core), cols(peer(k))].astype(jnp.float32) + sib[k].astype(jnp.float32)
        if k:
            part[k] = pair.astype(part.dtype)
            second[k] = remote(part.at[k], inbox.at[k], s2.at[k], r2.at[k], device_id=to(k))
            second[k].start()
        else:
            part[0] = pair.astype(part.dtype)
    for k in range(1, chips):
        second[k].wait_recv()
    total = part[0].astype(jnp.float32)
    for k in range(1, chips):
        total = total + inbox[k].astype(jnp.float32)
    out[rows(core), cols(chip)] = total.astype(out.dtype)

    mine = out.at[rows(core), cols(chip)]
    third = {}
    for k in range(1, chips):
        third[k] = remote(mine, mine, s3.at[k], r3.at[k], device_id=to(k))
        third[k].start()
    fourth = {0: remote(mine, mine, s4.at[0], r4.at[0], device_id=sibling)}
    fourth[0].start()
    for k in range(1, chips):
        third[k].wait_recv()
        landed = out.at[rows(core), cols(lax.rem(chip + chips - k, chips))]
        fourth[k] = remote(landed, landed, s4.at[k], r4.at[k], device_id=sibling)
        fourth[k].start()
    for k in range(chips):
        fourth[k].wait_recv()
        fourth[k].wait_send()
        first[k].wait_send()
        if k:
            second[k].wait_send()
            third[k].wait_send()


def replica_sum(snap, replicas):
    chips = replicas // CORES
    rows, cols = snap.shape
    piece = (chips, rows // CORES, cols // chips)
    dma = pltpu.SemaphoreType.DMA((chips,))
    return pl.pallas_call(
        functools.partial(sum_kernel, chips),
        out_shape=jax.ShapeDtypeStruct(snap.shape, snap.dtype),
        in_specs=[vmem_spec()],
        out_specs=vmem_spec(),
        scratch_shapes=[pltpu.VMEM(piece, snap.dtype)] * 3 + [dma] * 8,
        compiler_params=pltpu.CompilerParams(
            collective_id=0, has_side_effects=True, vmem_limit_bytes=16 * MIB
        ),
        cost_estimate=pl.CostEstimate(flops=0, bytes_accessed=48 * snap.size, transcendentals=0),
        name="replica_sum",
    )(snap)


def fragment_kernel(scale, total, outer, momentum, snap, local, due, outer_next, momentum_next, local_next):
    base, old = outer[...], momentum[...]
    pseudo = base - total[...].astype(jnp.float32) * scale
    moment = 0.9 * old + pseudo
    stepped = base - 0.7 * (pseudo + 0.9 * moment)
    keep = due[...] == 1
    outer_next[...] = jnp.where(keep, stepped, base)
    momentum_next[...] = jnp.where(keep, moment, old)
    here = local[...].astype(jnp.float32)
    merged = stepped + (here - snap[...].astype(jnp.float32))
    local_next[...] = jnp.where(keep, merged, here).astype(local_next.dtype)


def fragment(total, outer, momentum, snap, local, due, replicas):
    rows, cols = outer.shape
    step = 16
    spec = pl.BlockSpec((step, cols), lambda i: (i, 0))
    return pl.pallas_call(
        functools.partial(fragment_kernel, 1.0 / replicas),
        grid=(rows // step,),
        out_shape=[
            jax.ShapeDtypeStruct(outer.shape, outer.dtype),
            jax.ShapeDtypeStruct(outer.shape, outer.dtype),
            jax.ShapeDtypeStruct(local.shape, local.dtype),
        ],
        in_specs=[spec] * 5 + [pl.BlockSpec((step, 1), lambda i: (i, 0))],
        out_specs=[spec] * 3,
        compiler_params=pltpu.CompilerParams(vmem_limit_bytes=24 * MIB),
        cost_estimate=pl.CostEstimate(
            flops=12 * outer.size, bytes_accessed=24 * outer.size, transcendentals=0
        ),
        name="fragment_step",
    )(total, outer, momentum, snap, local, due.reshape(rows, 1))


def early_kernel(m, *refs):
    parts, left, right, xlt, dr = refs[:m], refs[m], refs[m + 1], refs[m + 2], refs[m + 3]
    rows = parts[0].shape[1]
    for k in range(m):
        span = slice(k * rows, (k + 1) * rows)
        xl = jnp.dot(parts[k][0], left[...], preferred_element_type=jnp.float32)
        xlt[:, span] = xl.T.astype(xlt.dtype)
        dr[span, :] = jnp.dot(
            parts[k][1], right[...], preferred_element_type=jnp.float32
        ).astype(dr.dtype)


def early(parts, left, right):
    m = len(parts)
    rows, width = parts[0].shape[1:]
    return pl.pallas_call(
        functools.partial(early_kernel, m),
        out_shape=[
            jax.ShapeDtypeStruct((width, m * rows), left.dtype),
            jax.ShapeDtypeStruct((m * rows, width), left.dtype),
        ],
        in_specs=[vmem_spec()] * (m + 2),
        out_specs=[vmem_spec()] * 2,
        compiler_params=pltpu.CompilerParams(vmem_limit_bytes=24 * MIB),
        cost_estimate=pl.CostEstimate(
            flops=4 * m * rows * width * width, bytes_accessed=8 * MIB, transcendentals=0
        ),
        name="early_products",
    )(*parts, left, right)


def tail_kernel(
    step, last, xlt_in, dr_in, left_in, right_in, first_in, second_in,
    update, first_next, second_next,
    tail, xlt, dr, left, right, first, second, first_out, second_out, back, up, sems, chunk_sems,
):
    width = left.shape[0]
    rows = tail.shape[1]
    done = dr_in.shape[0]
    chunks = [slice(k * step, (k + 1) * step) for k in range(width // step)]
    load = [
        pltpu.make_async_copy(last, tail, sems.at[0]),
        pltpu.make_async_copy(left_in, left, sems.at[1]),
        pltpu.make_async_copy(right_in, right, sems.at[2]),
        pltpu.make_async_copy(dr_in, dr.at[:done], sems.at[3]),
        pltpu.make_async_copy(xlt_in, xlt.at[:, :done], sems.at[4]),
    ]
    for copy in load:
        copy.start()
    firsts = [
        pltpu.make_async_copy(first_in.at[:, c], first.at[:, c], chunk_sems.at[0, k])
        for k, c in enumerate(chunks)
    ]
    seconds = [
        pltpu.make_async_copy(second_in.at[:, c], second.at[:, c], chunk_sems.at[1, k])
        for k, c in enumerate(chunks)
    ]
    for one, two in zip(firsts, seconds):
        one.start()
        two.start()
    load[0].wait()
    load[1].wait()
    xl = jnp.dot(tail[0], left[...], preferred_element_type=jnp.float32)
    xlt[:, done:] = xl.T.astype(xlt.dtype)
    load[2].wait()
    dr[done:, :] = jnp.dot(tail[1], right[...], preferred_element_type=jnp.float32).astype(dr.dtype)
    load[3].wait()
    load[4].wait()
    stores = []
    for k, c in enumerate(chunks):
        rotated = jnp.dot(xlt[...], dr[:, c], preferred_element_type=jnp.float32)
        firsts[k].wait()
        seconds[k].wait()
        one = 0.95 * first[:, c].astype(jnp.float32) + 0.05 * rotated
        two = 0.95 * second[:, c].astype(jnp.float32) + 0.05 * (rotated * rotated)
        first_out[:, c] = one.astype(first_out.dtype)
        second_out[:, c] = two.astype(second_out.dtype)
        stores.append(
            pltpu.make_async_copy(first_out.at[:, c], first_next.at[:, c], chunk_sems.at[2, k])
        )
        stores.append(
            pltpu.make_async_copy(second_out.at[:, c], second_next.at[:, c], chunk_sems.at[3, k])
        )
        stores[-2].start()
        stores[-1].start()
        scaled = CORRECT * two
        bottom = scaled * lax.rsqrt(scaled) + CORRECT * 1e-08
        guess = pl.reciprocal(bottom, approx=True)
        direction = (one * (guess * (2.0 - bottom * guess))).astype(jnp.bfloat16)
        back[:, c] = jnp.dot(left[...], direction, preferred_element_type=jnp.float32).astype(
            back.dtype
        )
    for k, c in enumerate(chunks):
        up[:, c] = lax.dot_general(
            back[...], right[c, :], (((1,), (1,)), ((), ())), preferred_element_type=jnp.float32
        ).astype(up.dtype)
        stores.append(pltpu.make_async_copy(up.at[:, c], update.at[:, c], chunk_sems.at[4, k]))
        stores[-1].start()
    for copy in stores:
        copy.wait()


def finish(last, xlt, dr, left, right, first, second):
    width = left.shape[0]
    rows = last.shape[1]
    tokens = dr.shape[0] + rows
    step = 256
    square = pltpu.VMEM((width, width), left.dtype)
    return pl.pallas_call(
        functools.partial(tail_kernel, step),
        out_shape=[jax.ShapeDtypeStruct((width, width), left.dtype)] * 3,
        in_specs=[any_spec()] * 7,
        out_specs=[any_spec()] * 3,
        scratch_shapes=[
            pltpu.VMEM(last.shape, last.dtype),
            pltpu.VMEM((width, tokens), left.dtype),
            pltpu.VMEM((tokens, width), left.dtype),
        ]
        + [square] * 8
        + [pltpu.SemaphoreType.DMA((5,)), pltpu.SemaphoreType.DMA((5, width // step))],
        compiler_params=pltpu.CompilerParams(vmem_limit_bytes=40 * MIB),
        cost_estimate=pl.CostEstimate(
            flops=6 * width**3, bytes_accessed=14 * MIB, transcendentals=2 * width * width
        ),
        name="soap_tail",
    )(last, xlt, dr, left, right, first, second)


def per_device(
    tokens,
    out_grads,
    block_ids,
    left_basis,
    right_basis,
    first_moment,
    second_moment,
    outer_params,
    outer_momentum,
    snapshot,
    local_params,
    due_rows,
):
    n = lax.axis_size("fsdp")
    replicas = lax.axis_size("replica")
    left, right = left_basis[0, 0], right_basis[0, 0]
    order = [0] + sorted(range(1, n), key=lambda s: abs(2 * s - n))
    sent = gather(tokens, out_grads, block_ids, left.shape[-1], n, order)
    parts = [sent[0]]
    for k in range(1, n):
        pairs = [(i, (i + order[k]) % n) for i in range(n)]
        parts.append(lax.ppermute(sent[k], "fsdp", pairs))
    total = replica_sum(snapshot[0], replicas)
    outer_next, momentum_next, local_next = fragment(
        total, outer_params, outer_momentum, snapshot[0], local_params[0], due_rows, replicas
    )
    xlt, dr = early(parts[:-1], left, right)
    update, first_next, second_next = finish(
        parts[-1], xlt, dr, left, right, first_moment[0, 0], second_moment[0, 0]
    )
    return (
        update[None, None],
        first_next[None, None],
        second_next[None, None],
        outer_next,
        momentum_next,
        local_next[None],
    )


def solution(mesh):
    return jax.shard_map(
        per_device,
        mesh=mesh,
        in_specs=(
            P(("replica", "fsdp"), None),
            P(("replica", "fsdp"), None),
            P(),
            P("replica", "fsdp", None, None),
            P("replica", "fsdp", None, None),
            P("replica", "fsdp", None, None),
            P("replica", "fsdp", None, None),
            P("fsdp", None),
            P("fsdp", None),
            P("replica", "fsdp", None),
            P("replica", "fsdp", None),
            P("fsdp"),
        ),
        out_specs=(
            P("replica", "fsdp", None, None),
            P("replica", "fsdp", None, None),
            P("replica", "fsdp", None, None),
            P("fsdp", None),
            P("fsdp", None),
            P("replica", "fsdp", None),
        ),
        check_vma=False,
    )
```

time: 110 us -> 70.7 us (0.64)
  the two profiles are of different devices: /device:TPU:11 before, /device:TPU:0 now
where the time goes in v2:
time: 70.7 us; the launch traced here: 70.5 us
  Pallas kernels  53.8 us (76%)
  local copies, waits for them, and re-layouts  7.98 us (11%)
  starting transfers between devices  7.93 us (11%)
  between operations  0.76 us (1%)
    pallas_call x1, Pallas kernels, replica_sum(): pl.pallas_call(functools.partial(sum_kernel, chips), out_shape=jax.ShapeD...  31.6 us
    pallas_call x1, Pallas kernels, finish(): pl.pallas_call(functools.partial(tail_kernel, step), out_shape=[jax.Shape...  11.5 us
    ppermute x3, starting transfers between devices, per_device(): parts.append(lax.ppermute(sent[k], 'fsdp', pairs))  7.93 us
    unnamed x24, local copies, waits for them, and re-layouts  7.87 us
    pallas_call x1, Pallas kernels, fragment(): pl.pallas_call(functools.partial(fragment_kernel, 1.0 / replicas), grid=(...  5.84 us
    pallas_call x1, Pallas kernels, early(): pl.pallas_call(functools.partial(early_kernel, m), out_shape=[jax.ShapeDt...  3.17 us
    pallas_call x1, Pallas kernels, gather(): pl.pallas_call(functools.partial(gather_kernel, n, width, out_grads.shape...  1.65 us
  transfers between devices with their start and end apart: 3, of which 0 were waited for; matrix products, arithmetic and copies ran while one was open for 0% of the time, Pallas kernels for 58%

profile of v2, /device:TPU:0, one launch (start us, length us, event | category | flops | bytes accessed | tf_op | source)
XLA Modules:
  0.0 70.5 jit_solution(31287629043476519)
XLA Ops:
  0.6 0.0 copy-start
  0.6 0.0 copy-start.3
  0.7 2.2 %copy-done.3 = bf16[128,14336]{1,0:T(8,128)(2,1)S(1)} copy-done((bf16[128,14336]{1,0:T(8,128)(2,1)S(1)}, bf16[128,14336]{1,0:T(8,128)(2,1)}, u32[]{:S(2)}) %copy-start.3) | copy-done | bytes 3670040
  2.8 0.0 copy-start.5
  2.8 1.2 %copy-done.5 = bf16[128,4096]{1,0:T(8,128)(2,1)S(1)} copy-done((bf16[128,4096]{1,0:T(8,128)(2,1)S(1)}, bf16[128,4096]{1,0:T(8,128)(2,1)}, u32[]{:S(2)}) %copy-start.5) | copy-done | bytes 1048600
  4.1 0.0 copy-start.6
  4.1 0.7 copy-done.6
  4.7 0.0 copy-start.11
  4.7 1.6 %gather_slots.1 = (bf16[2,128,1024]{2,1,0:T(8,128)(2,1)S(1)}, bf16[2,128,1024]{2,1,0:T(8,128)(2,1)}, bf16[2,128,1024]{2,1,0:T(8,128)(2,1)}, bf16[2,128,1024]{2,1,0:T(8,128)(2,1)S(1)}) custom-call(s32[4]{0:T(128)S(1)} %copy-done.6, bf16[128,4096]{1,0:T(8,128)(2,1)S(1)} %copy-done.5, bf16[128,14336]{1,0:T(8,128)(2,1)S(1)} %copy-done.3), custom_call_target="tpu_custom_call" | custom-call | bytes 8388608 | tf_op jit(solution)/shard_map/gather_slots/pallas_call | solution.py:45
  6.4 4.1 %collective-permute-start.1 = (bf16[2,128,1024]{2,1,0:T(8,128)(2,1)}, bf16[2,128,1024]{2,1,0:T(8,128)(2,1)}, u32[]{:S(2)}, u32[]{:S(2)}) collective-permute-start(bf16[2,128,1024]{2,1,0:T(8,128)(2,1)} %get-tuple-element.20), channel_id=1, source_target_pairs={{0,2},{1,3},{2,0},{3,1},{4,6},{5,7},{6,4},{7,5},{8,10},{9,11},{10,... | collective-permute-start | bytes 1572872 | tf_op jit(solution)/shard_map/ppermute | solution.py:336
  10.5 1.6 %collective-permute-start.2 = (bf16[2,128,1024]{2,1,0:T(8,128)(2,1)}, bf16[2,128,1024]{2,1,0:T(8,128)(2,1)}, u32[]{:S(2)}, u32[]{:S(2)}) collective-permute-start(bf16[2,128,1024]{2,1,0:T(8,128)(2,1)} %get-tuple-element.21), channel_id=1, source_target_pairs={{0,1},{1,2},{2,3},{3,0},{4,5},{5,6},{6,7},{7,4},{8,9},{9,10},{10,1... | collective-permute-start | bytes 1572872 | tf_op jit(solution)/shard_map/ppermute | solution.py:336
  12.0 2.2 %collective-permute-start = (bf16[2,128,1024]{2,1,0:T(8,128)(2,1)S(1)}, bf16[2,128,1024]{2,1,0:T(8,128)(2,1)}, u32[]{:S(2)}, u32[]{:S(2)}) collective-permute-start(bf16[2,128,1024]{2,1,0:T(8,128)(2,1)S(1)} %get-tuple-element.18), channel_id=1, source_target_pairs={{0,3},{1,0},{2,1},{3,2},{4,7},{5,4},{6,5},{7,6},{8,11},{9,8},{10,9... | collective-permute-start | bytes 1572872 | tf_op jit(solution)/shard_map/ppermute | solution.py:336
  14.3 0.0 copy-done.11
  14.3 0.1 copy.18.due
  14.4 0.0 copy-done
  14.4 0.0 copy-start.1
  14.4 31.6 %replica_sum.1.total = bf16[128,8192]{1,0:T(8,128)(2,1)S(1)} custom-call(bf16[128,8192]{1,0:T(8,128)(2,1)S(1)} %bitcast.11), custom_call_target="tpu_custom_call" | custom-call | bytes 50331648 | tf_op jit(solution)/shard_map/replica_sum/pallas_call | solution.py:137
  46.1 0.0 copy-done.1
  46.1 0.0 copy-start.2
  46.1 2.2 %copy-done.2 = f32[128,8192]{1,0:T(8,128)S(1)} copy-done((f32[128,8192]{1,0:T(8,128)S(1)}, f32[128,8192]{1,0:T(8,128)}, u32[]{:S(2)}) %copy-start.2) | copy-done | bytes 4194328
  48.3 0.0 copy-start.4
  48.3 1.6 %copy-done.4 = bf16[1,128,8192]{2,1,0:T(8,128)(2,1)S(1)} copy-done((bf16[1,128,8192]{2,1,0:T(8,128)(2,1)S(1)}, bf16[1,128,8192]{2,1,0:T(8,128)(2,1)}, u32[]{:S(2)}) %copy-start.4) | copy-done | bytes 2097176
  49.9 0.0 copy-start.7
  49.9 0.0 copy-start.8
  49.9 5.8 %fragment_step.1 = (f32[128,8192]{1,0:T(8,128)}, f32[128,8192]{1,0:T(8,128)}, bf16[128,8192]{1,0:T(8,128)(2,1)}) custom-call(bf16[128,8192]{1,0:T(8,128)(2,1)S(1)} %replica_sum.1.total, f32[128,8192]{1,0:T(8,128)S(1)} %copy-done.1, f32[128,8192]{1,0:T(8,128)S(1)} %copy-done.2, bf16[128,8192]{1,0:T(8,128)(2,1)S(1)} %bitcast.12, ...), custom_call_target="tpu_custom_call" | custom-call | flops 12582912 | bytes 25165824 | tf_op jit(solution)/shard_map/fragment_step/pallas_call | solution.py:168
  55.7 0.0 collective-permute-done.1.refs_1_
  55.7 0.0 collective-permute-done.2.refs_2_
  55.7 0.0 copy-done.7
  55.7 0.0 copy-done.8
  55.7 0.0 copy-start.9
  55.7 0.0 copy-start.10
  55.8 3.2 %early_products.1 = (bf16[1024,384]{1,0:T(8,128)(2,1)S(1)}, bf16[384,1024]{1,0:T(8,128)(2,1)S(1)}) custom-call(bf16[2,128,1024]{2,1,0:T(8,128)(2,1)S(1)} %get-tuple-element.19.refs_0_, bf16[2,128,1024]{2,1,0:T(8,128)(2,1)} %collective-permute-done.1.refs_1_, bf16[2,128,1024]{2,1,0:T(8,128)(2,1)} %collective-permute-done.2.refs_2_, ...), custom_call_target="tpu_custom_call" | custom-call | flops 1610612736 | bytes 8388608 | tf_op jit(solution)/shard_map/early_products/pallas_call | solution.py:201
  58.9 0.0 collective-permute-done.last
  58.9 0.0 copy-done.9
  59.0 0.0 copy-done.10
  59.0 11.5 %soap_tail.1 = (bf16[1024,1024]{1,0:T(8,128)(2,1)}, bf16[1024,1024]{1,0:T(8,128)(2,1)}, bf16[1024,1024]{1,0:T(8,128)(2,1)}) custom-call(bf16[2,128,1024]{2,1,0:T(8,128)(2,1)} %collective-permute-done.last, bf16[1024,384]{1,0:T(8,128)(2,1)S(1)} %get-tuple-element.22.xlt_in, bf16[384,1024]{1,0:T(8,128)(2,1)S(1)} %get-tuple-element.23.dr_in, ...), custom_call_target="tpu_custom_call" | custom-call | flops 6442450944 | bytes 14680064 | tf_op jit(solution)/shard_map/soap_tail/pallas_call | solution.py:294
Async XLA Ops:
  0.6 13.8 %copy-start = (bf16[1,128,8192]{2,1,0:T(8,128)(2,1)S(1)}, bf16[1,128,8192]{2,1,0:T(8,128)(2,1)}, u32[]{:S(2)}) copy-start(bf16[1,128,8192]{2,1,0:T(8,128)(2,1)} %param.21) | copy-start | bytes 6291460
  0.6 2.2 %copy-start.3 = (bf16[128,14336]{1,0:T(8,128)(2,1)S(1)}, bf16[128,14336]{1,0:T(8,128)(2,1)}, u32[]{:S(2)}) copy-start(bf16[128,14336]{1,0:T(8,128)(2,1)} %out_grads.1) | copy-start | bytes 11010052
  2.8 1.2 %copy-start.5 = (bf16[128,4096]{1,0:T(8,128)(2,1)S(1)}, bf16[128,4096]{1,0:T(8,128)(2,1)}, u32[]{:S(2)}) copy-start(bf16[128,4096]{1,0:T(8,128)(2,1)} %tokens.1) | copy-start | bytes 3145732
  4.1 0.7 copy-start.6
  4.7 9.6 %copy-start.11 = (s32[128]{0:T(128)S(1)}, s32[128]{0:T(128)}, u32[]{:S(2)}) copy-start(s32[128]{0:T(128)} %param.23) | copy-start | bytes 1540
  6.4 49.3 %collective-permute-start.1 = (bf16[2,128,1024]{2,1,0:T(8,128)(2,1)}, bf16[2,128,1024]{2,1,0:T(8,128)(2,1)}, u32[]{:S(2)}, u32[]{:S(2)}) collective-permute-start(bf16[2,128,1024]{2,1,0:T(8,128)(2,1)} %get-tuple-element.20), channel_id=1, source_target_pairs={{0,2},{1,3},{2,0},{3,1},{4,6},{5,7},{6,4},{7,5},{8,10},{9,11},{10,... | collective-permute-start | bytes 1572872 | tf_op jit(solution)/shard_map/ppermute | solution.py:336
  10.5 45.2 %collective-permute-start.2 = (bf16[2,128,1024]{2,1,0:T(8,128)(2,1)}, bf16[2,128,1024]{2,1,0:T(8,128)(2,1)}, u32[]{:S(2)}, u32[]{:S(2)}) collective-permute-start(bf16[2,128,1024]{2,1,0:T(8,128)(2,1)} %get-tuple-element.21), channel_id=1, source_target_pairs={{0,1},{1,2},{2,3},{3,0},{4,5},{5,6},{6,7},{7,4},{8,9},{9,10},{10,1... | collective-permute-start | bytes 1572872 | tf_op jit(solution)/shard_map/ppermute | solution.py:336
  12.0 46.9 %collective-permute-start = (bf16[2,128,1024]{2,1,0:T(8,128)(2,1)S(1)}, bf16[2,128,1024]{2,1,0:T(8,128)(2,1)}, u32[]{:S(2)}, u32[]{:S(2)}) collective-permute-start(bf16[2,128,1024]{2,1,0:T(8,128)(2,1)S(1)} %get-tuple-element.18), channel_id=1, source_target_pairs={{0,3},{1,0},{2,1},{3,2},{4,7},{5,4},{6,5},{7,6},{8,11},{9,8},{10,9... | collective-permute-start | bytes 1572872 | tf_op jit(solution)/shard_map/ppermute | solution.py:336
  14.4 31.7 %copy-start.1 = (f32[128,8192]{1,0:T(8,128)S(1)}, f32[128,8192]{1,0:T(8,128)}, u32[]{:S(2)}) copy-start(f32[128,8192]{1,0:T(8,128)} %outer.1) | copy-start | bytes 12582916
  46.1 2.2 %copy-start.2 = (f32[128,8192]{1,0:T(8,128)S(1)}, f32[128,8192]{1,0:T(8,128)}, u32[]{:S(2)}) copy-start(f32[128,8192]{1,0:T(8,128)} %momentum.1) | copy-start | bytes 12582916
  48.3 1.6 %copy-start.4 = (bf16[1,128,8192]{2,1,0:T(8,128)(2,1)S(1)}, bf16[1,128,8192]{2,1,0:T(8,128)(2,1)}, u32[]{:S(2)}) copy-start(bf16[1,128,8192]{2,1,0:T(8,128)(2,1)} %param.22) | copy-start | bytes 6291460
  49.9 5.9 %copy-start.7 = (bf16[1,1,1024,1024]{3,2,1,0:T(8,128)(2,1)S(1)}, bf16[1,1,1024,1024]{3,2,1,0:T(8,128)(2,1)}, u32[]{:S(2)}) copy-start(bf16[1,1,1024,1024]{3,2,1,0:T(8,128)(2,1)} %param.15) | copy-start | bytes 6291460
  49.9 5.9 %copy-start.8 = (bf16[1,1,1024,1024]{3,2,1,0:T(8,128)(2,1)S(1)}, bf16[1,1,1024,1024]{3,2,1,0:T(8,128)(2,1)}, u32[]{:S(2)}) copy-start(bf16[1,1,1024,1024]{3,2,1,0:T(8,128)(2,1)} %param.16) | copy-start | bytes 6291460
  55.7 3.2 %copy-start.9 = (bf16[1,1,1024,1024]{3,2,1,0:T(8,128)(2,1)S(1)}, bf16[1,1,1024,1024]{3,2,1,0:T(8,128)(2,1)}, u32[]{:S(2)}) copy-start(bf16[1,1,1024,1024]{3,2,1,0:T(8,128)(2,1)} %param.17) | copy-start | bytes 6291460
  55.7 3.2 %copy-start.10 = (bf16[1,1,1024,1024]{3,2,1,0:T(8,128)(2,1)S(1)}, bf16[1,1,1024,1024]{3,2,1,0:T(8,128)(2,1)}, u32[]{:S(2)}) copy-start(bf16[1,1,1024,1024]{3,2,1,0:T(8,128)(2,1)} %param.18) | copy-start | bytes 6291460

commit v3 on v2

--- a/solution.py
+++ b/solution.py
@@ -14,6 +14,10 @@
 
 def any_spec():
     return pl.BlockSpec(memory_space=pl.ANY)
+
+
+def hbm_spec():
+    return pl.BlockSpec(memory_space=pltpu.HBM)
 
 
 def vmem_spec():
@@ -45,10 +49,10 @@
     return pl.pallas_call(
         functools.partial(gather_kernel, n, width, out_grads.shape[1] // width, order),
         out_shape=[jax.ShapeDtypeStruct((2, rows, width), tokens.dtype)] * n,
-        in_specs=[pl.BlockSpec(memory_space=pltpu.SMEM), any_spec(), any_spec()],
+        in_specs=[pl.BlockSpec(memory_space=pltpu.SMEM), hbm_spec(), hbm_spec()],
         out_specs=[any_spec()] * n,
         scratch_shapes=[pltpu.SemaphoreType.DMA((2, n))],
-        compiler_params=pltpu.CompilerParams(vmem_limit_bytes=4 * MIB),
+        compiler_params=pltpu.CompilerParams(vmem_limit_bytes=60 * MIB),
         cost_estimate=pl.CostEstimate(flops=0, bytes_accessed=16 * n * rows * width, transcendentals=0),
         name="gather_slots",
     )(block_ids, tokens, out_grads)
@@ -143,41 +147,58 @@
         compiler_params=pltpu.CompilerParams(
             collective_id=0, has_side_effects=True, vmem_limit_bytes=16 * MIB
         ),
-        cost_estimate=pl.CostEstimate(flops=0, bytes_accessed=48 * snap.size, transcendentals=0),
+        cost_estimate=pl.CostEstimate(flops=0, bytes_accessed=100 * snap.size, transcendentals=0),
         name="replica_sum",
     )(snap)
 
 
-def fragment_kernel(scale, total, outer, momentum, snap, local, due, outer_next, momentum_next, local_next):
-    base, old = outer[...], momentum[...]
-    pseudo = base - total[...].astype(jnp.float32) * scale
-    moment = 0.9 * old + pseudo
-    stepped = base - 0.7 * (pseudo + 0.9 * moment)
-    keep = due[...] == 1
-    outer_next[...] = jnp.where(keep, stepped, base)
-    momentum_next[...] = jnp.where(keep, moment, old)
-    here = local[...].astype(jnp.float32)
-    merged = stepped + (here - snap[...].astype(jnp.float32))
-    local_next[...] = jnp.where(keep, merged, here).astype(local_next.dtype)
+def fragment_kernel(
+    step, scale, total, outer, momentum, snap, local, due, outer_next, momentum_next, local_next,
+    outer_out, momentum_out, local_out, sems,
+):
+    stores = []
+    for k in range(outer.shape[0] // step):
+        r = slice(k * step, (k + 1) * step)
+        base, old = outer[r, :], momentum[r, :]
+        pseudo = base - total[r, :].astype(jnp.float32) * scale
+        moment = 0.9 * old + pseudo
+        stepped = base - 0.7 * (pseudo + 0.9 * moment)
+        keep = due[r, :] == 1
+        outer_out[r, :] = jnp.where(keep, stepped, base)
+        momentum_out[r, :] = jnp.where(keep, moment, old)
+        here = local[r, :].astype(jnp.float32)
+        merged = stepped + (here - snap[r, :].astype(jnp.float32))
+        local_out[r, :] = jnp.where(keep, merged, here).astype(local_out.dtype)
+        for m, (src, dst) in enumerate(
+            ((outer_out, outer_next), (momentum_out, momentum_next), (local_out, local_next))
+        ):
+            stores.append(pltpu.make_async_copy(src.at[r], dst.at[r], sems.at[m, k]))
+            stores[-1].start()
+    for copy in stores:
+        copy.wait()
 
 
 def fragment(total, outer, momentum, snap, local, due, replicas):
     rows, cols = outer.shape
     step = 16
-    spec = pl.BlockSpec((step, cols), lambda i: (i, 0))
-    return pl.pallas_call(
-        functools.partial(fragment_kernel, 1.0 / replicas),
-        grid=(rows // step,),
+    return pl.pallas_call(
+        functools.partial(fragment_kernel, step, 1.0 / replicas),
         out_shape=[
             jax.ShapeDtypeStruct(outer.shape, outer.dtype),
             jax.ShapeDtypeStruct(outer.shape, outer.dtype),
             jax.ShapeDtypeStruct(local.shape, local.dtype),
         ],
-        in_specs=[spec] * 5 + [pl.BlockSpec((step, 1), lambda i: (i, 0))],
-        out_specs=[spec] * 3,
-        compiler_params=pltpu.CompilerParams(vmem_limit_bytes=24 * MIB),
+        in_specs=[vmem_spec()] * 6,
+        out_specs=[hbm_spec()] * 3,
+        scratch_shapes=[
+            pltpu.VMEM(outer.shape, outer.dtype),
+            pltpu.VMEM(outer.shape, outer.dtype),
+            pltpu.VMEM(local.shape, local.dtype),
+            pltpu.SemaphoreType.DMA((3, rows // step)),
+        ],
+        compiler_params=pltpu.CompilerParams(vmem_limit_bytes=16 * MIB),
         cost_estimate=pl.CostEstimate(
-            flops=12 * outer.size, bytes_accessed=24 * outer.size, transcendentals=0
+            flops=12 * outer.size, bytes_accessed=16 * outer.size, transcendentals=0
         ),
         name="fragment_step",
     )(total, outer, momentum, snap, local, due.reshape(rows, 1))
@@ -206,7 +227,7 @@
         ],
         in_specs=[vmem_spec()] * (m + 2),
         out_specs=[vmem_spec()] * 2,
-        compiler_params=pltpu.CompilerParams(vmem_limit_bytes=24 * MIB),
+        compiler_params=pltpu.CompilerParams(vmem_limit_bytes=16 * MIB),
         cost_estimate=pl.CostEstimate(
             flops=4 * m * rows * width * width, bytes_accessed=8 * MIB, transcendentals=0
         ),
@@ -214,60 +235,45 @@
     )(*parts, left, right)
 
 
-def tail_kernel(
-    step, last, xlt_in, dr_in, left_in, right_in, first_in, second_in,
-    update, first_next, second_next,
-    tail, xlt, dr, left, right, first, second, first_out, second_out, back, up, sems, chunk_sems,
-):
-    width = left.shape[0]
-    rows = tail.shape[1]
+def tail_kernel(step, m, *refs):
+    parts = refs[:m]
+    (
+        xlt_in, dr_in, left, right, first, second, update, first_next, second_next,
+        xlt, dr, first_out, second_out, back, up, sems,
+    ) = refs[m:]
     done = dr_in.shape[0]
-    chunks = [slice(k * step, (k + 1) * step) for k in range(width // step)]
-    load = [
-        pltpu.make_async_copy(last, tail, sems.at[0]),
-        pltpu.make_async_copy(left_in, left, sems.at[1]),
-        pltpu.make_async_copy(right_in, right, sems.at[2]),
-        pltpu.make_async_copy(dr_in, dr.at[:done], sems.at[3]),
-        pltpu.make_async_copy(xlt_in, xlt.at[:, :done], sems.at[4]),
-    ]
-    for copy in load:
-        copy.start()
-    firsts = [
-        pltpu.make_async_copy(first_in.at[:, c], first.at[:, c], chunk_sems.at[0, k])
-        for k, c in enumerate(chunks)
-    ]
-    seconds = [
-        pltpu.make_async_copy(second_in.at[:, c], second.at[:, c], chunk_sems.at[1, k])
-        for k, c in enumerate(chunks)
-    ]
-    for one, two in zip(firsts, seconds):
-        one.start()
-        two.start()
-    load[0].wait()
-    load[1].wait()
-    xl = jnp.dot(tail[0], left[...], preferred_element_type=jnp.float32)
+    chunks = [slice(k * step, (k + 1) * step) for k in range(left.shape[0] // step)]
+    xl = jnp.dot(
+        jnp.concatenate([part[0] for part in parts]),
+        left[...],
+        preferred_element_type=jnp.float32,
+    )
+    xlt[:, :done] = xlt_in[...]
     xlt[:, done:] = xl.T.astype(xlt.dtype)
-    load[2].wait()
-    dr[done:, :] = jnp.dot(tail[1], right[...], preferred_element_type=jnp.float32).astype(dr.dtype)
-    load[3].wait()
-    load[4].wait()
+    dr[:done, :] = dr_in[...]
+    grads = jnp.concatenate([part[1] for part in parts])
+
+    def rotate(c):
+        dr[done:, c] = jnp.dot(
+            grads, right[:, c], preferred_element_type=jnp.float32
+        ).astype(dr.dtype)
+        return jnp.dot(xlt[...], dr[:, c], preferred_element_type=jnp.float32)
+
     stores = []
+
+    def store(src, dst, c, which, k):
+        stores.append(pltpu.make_async_copy(src.at[:, c], dst.at[:, c], sems.at[which, k]))
+        stores[-1].start()
+
+    ahead = rotate(chunks[0])
     for k, c in enumerate(chunks):
-        rotated = jnp.dot(xlt[...], dr[:, c], preferred_element_type=jnp.float32)
-        firsts[k].wait()
-        seconds[k].wait()
+        rotated = ahead
+        if k + 1 < len(chunks):
+            ahead = rotate(chunks[k + 1])
         one = 0.95 * first[:, c].astype(jnp.float32) + 0.05 * rotated
         two = 0.95 * second[:, c].astype(jnp.float32) + 0.05 * (rotated * rotated)
         first_out[:, c] = one.astype(first_out.dtype)
         second_out[:, c] = two.astype(second_out.dtype)
-        stores.append(
-            pltpu.make_async_copy(first_out.at[:, c], first_next.at[:, c], chunk_sems.at[2, k])
-        )
-        stores.append(
-            pltpu.make_async_copy(second_out.at[:, c], second_next.at[:, c], chunk_sems.at[3, k])
-        )
-        stores[-2].start()
-        stores[-1].start()
         scaled = CORRECT * two
         bottom = scaled * lax.rsqrt(scaled) + CORRECT * 1e-08
         guess = pl.reciprocal(bottom, approx=True)
@@ -275,40 +281,41 @@
         back[:, c] = jnp.dot(left[...], direction, preferred_element_type=jnp.float32).astype(
             back.dtype
         )
+        store(first_out, first_next, c, 0, k)
+        store(second_out, second_next, c, 1, k)
     for k, c in enumerate(chunks):
         up[:, c] = lax.dot_general(
             back[...], right[c, :], (((1,), (1,)), ((), ())), preferred_element_type=jnp.float32
         ).astype(up.dtype)
-        stores.append(pltpu.make_async_copy(up.at[:, c], update.at[:, c], chunk_sems.at[4, k]))
-        stores[-1].start()
+        store(up, update, c, 2, k)
     for copy in stores:
         copy.wait()
 
 
-def finish(last, xlt, dr, left, right, first, second):
+def finish(parts, xlt, dr, left, right, first, second):
+    m = len(parts)
     width = left.shape[0]
-    rows = last.shape[1]
-    tokens = dr.shape[0] + rows
+    rows = parts[0].shape[1]
+    tokens = dr.shape[0] + m * rows
     step = 256
     square = pltpu.VMEM((width, width), left.dtype)
     return pl.pallas_call(
-        functools.partial(tail_kernel, step),
+        functools.partial(tail_kernel, step, m),
         out_shape=[jax.ShapeDtypeStruct((width, width), left.dtype)] * 3,
-        in_specs=[any_spec()] * 7,
-        out_specs=[any_spec()] * 3,
+        in_specs=[vmem_spec()] * (m + 6),
+        out_specs=[hbm_spec()] * 3,
         scratch_shapes=[
-            pltpu.VMEM(last.shape, last.dtype),
             pltpu.VMEM((width, tokens), left.dtype),
             pltpu.VMEM((tokens, width), left.dtype),
         ]
-        + [square] * 8
-        + [pltpu.SemaphoreType.DMA((5,)), pltpu.SemaphoreType.DMA((5, width // step))],
-        compiler_params=pltpu.CompilerParams(vmem_limit_bytes=40 * MIB),
+        + [square] * 4
+        + [pltpu.SemaphoreType.DMA((3, width // step))],
+        compiler_params=pltpu.CompilerParams(vmem_limit_bytes=32 * MIB),
         cost_estimate=pl.CostEstimate(
             flops=6 * width**3, bytes_accessed=14 * MIB, transcendentals=2 * width * width
         ),
         name="soap_tail",
-    )(last, xlt, dr, left, right, first, second)
+    )(*parts, xlt, dr, left, right, first, second)
 
 
 def per_device(
@@ -338,9 +345,9 @@
     outer_next, momentum_next, local_next = fragment(
         total, outer_params, outer_momentum, snapshot[0], local_params[0], due_rows, replicas
     )
-    xlt, dr = early(parts[:-1], left, right)
+    xlt, dr = early(parts[: n // 2], left, right)
     update, first_next, second_next = finish(
-        parts[-1], xlt, dr, left, right, first_moment[0, 0], second_moment[0, 0]
+        parts[n // 2 :], xlt, dr, left, right, first_moment[0, 0], second_moment[0, 0]
     )
     return (
         update[None, None],

time: 70.7 us -> 128 us (1.81)
  Pallas kernels: 53.8 us -> 114 us
  local copies, waits for them, and re-layouts: 7.98 us -> 4.82 us
    pallas_call x1, Pallas kernels: 1.65 us -> 65.5 us  [gather(): pl.pallas_call(functools.partial(gather_kernel, n, width, out_grads.shape...]
    unnamed x24 -> x20, local copies, waits for them, and re-layouts: 7.87 us -> 4.71 us
    pallas_call x1, Pallas kernels: 3.17 us -> 1.27 us  [early(): pl.pallas_call(functools.partial(early_kernel, m), out_shape=[jax.ShapeDt...]
    pallas_call x2, Pallas kernels: 17.3 us -> 15.8 us  [the longest x1 9.94 us: finish(): pl.pallas_call(functools.partial(tail_kernel, step, m), out_shape=[jax.Sh...]
  transfers between devices with their start and end apart: 3 -> 3, of which waited for: 0 -> 0; matrix products, arithmetic and copies ran while one was open for 0% -> 0% of each run, Pallas kernels for 58% -> 30%
where the time goes in v3:
time: 128 us
  Pallas kernels  114 us (89%)
  starting transfers between devices  7.93 us (6%)
  local copies, waits for them, and re-layouts  4.82 us (4%)
    pallas_call x1, Pallas kernels, gather(): pl.pallas_call(functools.partial(gather_kernel, n, width, out_grads.shape...  65.5 us
    pallas_call x1, Pallas kernels, replica_sum(): pl.pallas_call(functools.partial(sum_kernel, chips), out_shape=jax.ShapeD...  31.6 us
    pallas_call x1, Pallas kernels, finish(): pl.pallas_call(functools.partial(tail_kernel, step, m), out_shape=[jax.Sh...  9.94 us
    ppermute x3, starting transfers between devices, per_device(): parts.append(lax.ppermute(sent[k], 'fsdp', pairs))  7.93 us
    pallas_call x1, Pallas kernels, fragment(): pl.pallas_call(functools.partial(fragment_kernel, step, 1.0 / replicas),...  5.88 us
    unnamed x20, local copies, waits for them, and re-layouts  4.71 us
  transfers between devices with their start and end apart: 3, of which 0 were waited for; matrix products, arithmetic and copies ran while one was open for 0% of the time, Pallas kernels for 30%

profile of v3, /device:TPU:0, one launch (start us, length us, event | category | flops | bytes accessed | tf_op | source)
XLA Modules:
  0.0 127.8 jit_solution(5947004635867501290)
XLA Ops:
  0.6 0.0 copy-start.9
  0.6 0.0 copy-start
  0.7 65.5 %gather_slots.1 = (bf16[2,128,1024]{2,1,0:T(8,128)(2,1)}, bf16[2,128,1024]{2,1,0:T(8,128)(2,1)}, bf16[2,128,1024]{2,1,0:T(8,128)(2,1)}, bf16[2,128,1024]{2,1,0:T(8,128)(2,1)}) custom-call(s32[4]{0:T(128)} %ids.1, bf16[128,4096]{1,0:T(8,128)(2,1)} %tokens.1, bf16[128,14336]{1,0:T(8,128)(2,1)} %out_grads.1), custom_call_target="tpu_custom_call" | custom-call | bytes 8388608 | tf_op jit(solution)/shard_map/gather_slots/pallas_call | solution.py:49
  66.2 4.1 %collective-permute-start.2 = (bf16[2,128,1024]{2,1,0:T(8,128)(2,1)}, bf16[2,128,1024]{2,1,0:T(8,128)(2,1)S(1)}, u32[]{:S(2)}, u32[]{:S(2)}) collective-permute-start(bf16[2,128,1024]{2,1,0:T(8,128)(2,1)} %get-tuple-element.21), channel_id=1, source_target_pairs={{0,2},{1,3},{2,0},{3,1},{4,6},{5,7},{6,4},{7,5},{8,10},{9,11},{10,... | collective-permute-start | bytes 1572872 | tf_op jit(solution)/shard_map/ppermute | solution.py:343
  70.3 1.6 %collective-permute-start = (bf16[2,128,1024]{2,1,0:T(8,128)(2,1)}, bf16[2,128,1024]{2,1,0:T(8,128)(2,1)S(1)}, u32[]{:S(2)}, u32[]{:S(2)}) collective-permute-start(bf16[2,128,1024]{2,1,0:T(8,128)(2,1)} %get-tuple-element.18), channel_id=1, source_target_pairs={{0,1},{1,2},{2,3},{3,0},{4,5},{5,6},{6,7},{7,4},{8,9},{9,10},{10,1... | collective-permute-start | bytes 1572872 | tf_op jit(solution)/shard_map/ppermute | solution.py:343
  71.9 2.2 %collective-permute-start.1 = (bf16[2,128,1024]{2,1,0:T(8,128)(2,1)}, bf16[2,128,1024]{2,1,0:T(8,128)(2,1)}, u32[]{:S(2)}, u32[]{:S(2)}) collective-permute-start(bf16[2,128,1024]{2,1,0:T(8,128)(2,1)} %get-tuple-element.19), channel_id=1, source_target_pairs={{0,3},{1,0},{2,1},{3,2},{4,7},{5,4},{6,5},{7,6},{8,11},{9,8},{10,9... | collective-permute-start | bytes 1572872 | tf_op jit(solution)/shard_map/ppermute | solution.py:343
  74.1 0.0 copy-done.9
  74.1 0.1 copy.18.due
  74.2 0.0 copy-done
  74.2 0.0 copy-start.1
  74.2 31.6 %replica_sum.1.total = bf16[128,8192]{1,0:T(8,128)(2,1)S(1)} custom-call(bf16[128,8192]{1,0:T(8,128)(2,1)S(1)} %bitcast.11), custom_call_target="tpu_custom_call" | custom-call | bytes 104857600 | tf_op jit(solution)/shard_map/replica_sum/pallas_call | solution.py:141
  105.9 0.0 copy-done.1
  105.9 0.0 copy-start.2
  105.9 2.2 %copy-done.2 = f32[128,8192]{1,0:T(8,128)S(1)} copy-done((f32[128,8192]{1,0:T(8,128)S(1)}, f32[128,8192]{1,0:T(8,128)}, u32[]{:S(2)}) %copy-start.2) | copy-done | bytes 4194328
  108.1 0.0 copy-start.3
  108.1 1.6 %copy-done.3 = bf16[1,128,8192]{2,1,0:T(8,128)(2,1)S(1)} copy-done((bf16[1,128,8192]{2,1,0:T(8,128)(2,1)S(1)}, bf16[1,128,8192]{2,1,0:T(8,128)(2,1)}, u32[]{:S(2)}) %copy-start.3) | copy-done | bytes 2097176
  109.7 0.0 copy-start.4
  109.7 0.0 copy-start.5
  109.7 0.0 copy-start.6
  109.7 5.9 %fragment_step.1 = (f32[128,8192]{1,0:T(8,128)}, f32[128,8192]{1,0:T(8,128)}, bf16[128,8192]{1,0:T(8,128)(2,1)}) custom-call(bf16[128,8192]{1,0:T(8,128)(2,1)S(1)} %replica_sum.1.total, f32[128,8192]{1,0:T(8,128)S(1)} %copy-done.1, f32[128,8192]{1,0:T(8,128)S(1)} %copy-done.2, bf16[128,8192]{1,0:T(8,128)(2,1)S(1)} %bitcast.12, ...), custom_call_target="tpu_custom_call" | custom-call | flops 12582912 | bytes 16777216 | tf_op jit(solution)/shard_map/fragment_step/pallas_call | solution.py:184
  115.6 0.0 collective-permute-done.2.refs_1_
  115.6 0.0 copy-done.4
  115.6 0.0 copy-done.5
  115.6 0.0 copy-done.6
  115.6 0.0 copy-start.7
  115.6 0.0 copy-start.8
  115.6 1.3 early_products.1
  116.9 0.0 collective-permute-done.refs_0_
  116.9 0.0 collective-permute-done.1.refs_1_
  116.9 0.3 copy-done.7
  117.2 0.6 copy-done.8
  117.8 9.9 %soap_tail.1 = (bf16[1024,1024]{1,0:T(8,128)(2,1)}, bf16[1024,1024]{1,0:T(8,128)(2,1)}, bf16[1024,1024]{1,0:T(8,128)(2,1)}) custom-call(bf16[2,128,1024]{2,1,0:T(8,128)(2,1)S(1)} %collective-permute-done.refs_0_, bf16[2,128,1024]{2,1,0:T(8,128)(2,1)} %collective-permute-done.1.refs_1_, bf16[1024,256]{1,0:T(8,128)(2,1)S(1)} %get-tuple-element.22.refs_2_, ...), custom_call_target="tpu_custom_call" | custom-call | flops 6442450944 | bytes 14680064 | tf_op jit(solution)/shard_map/soap_tail/pallas_call | solution.py:302
Async XLA Ops:
  0.6 73.5 %copy-start.9 = (s32[128]{0:T(128)S(1)}, s32[128]{0:T(128)}, u32[]{:S(2)}) copy-start(s32[128]{0:T(128)} %param.23) | copy-start | bytes 1540
  0.6 73.6 %copy-start = (bf16[1,128,8192]{2,1,0:T(8,128)(2,1)S(1)}, bf16[1,128,8192]{2,1,0:T(8,128)(2,1)}, u32[]{:S(2)}) copy-start(bf16[1,128,8192]{2,1,0:T(8,128)(2,1)} %param.21) | copy-start | bytes 6291460
  66.2 49.4 %collective-permute-start.2 = (bf16[2,128,1024]{2,1,0:T(8,128)(2,1)}, bf16[2,128,1024]{2,1,0:T(8,128)(2,1)S(1)}, u32[]{:S(2)}, u32[]{:S(2)}) collective-permute-start(bf16[2,128,1024]{2,1,0:T(8,128)(2,1)} %get-tuple-element.21), channel_id=1, source_target_pairs={{0,2},{1,3},{2,0},{3,1},{4,6},{5,7},{6,4},{7,5},{8,10},{9,11},{10,... | collective-permute-start | bytes 1572872 | tf_op jit(solution)/shard_map/ppermute | solution.py:343
  70.3 46.6 %collective-permute-start = (bf16[2,128,1024]{2,1,0:T(8,128)(2,1)}, bf16[2,128,1024]{2,1,0:T(8,128)(2,1)S(1)}, u32[]{:S(2)}, u32[]{:S(2)}) collective-permute-start(bf16[2,128,1024]{2,1,0:T(8,128)(2,1)} %get-tuple-element.18), channel_id=1, source_target_pairs={{0,1},{1,2},{2,3},{3,0},{4,5},{5,6},{6,7},{7,4},{8,9},{9,10},{10,1... | collective-permute-start | bytes 1572872 | tf_op jit(solution)/shard_map/ppermute | solution.py:343
  71.9 45.1 %collective-permute-start.1 = (bf16[2,128,1024]{2,1,0:T(8,128)(2,1)}, bf16[2,128,1024]{2,1,0:T(8,128)(2,1)}, u32[]{:S(2)}, u32[]{:S(2)}) collective-permute-start(bf16[2,128,1024]{2,1,0:T(8,128)(2,1)} %get-tuple-element.19), channel_id=1, source_target_pairs={{0,3},{1,0},{2,1},{3,2},{4,7},{5,4},{6,5},{7,6},{8,11},{9,8},{10,9... | collective-permute-start | bytes 1572872 | tf_op jit(solution)/shard_map/ppermute | solution.py:343
  74.2 31.7 %copy-start.1 = (f32[128,8192]{1,0:T(8,128)S(1)}, f32[128,8192]{1,0:T(8,128)}, u32[]{:S(2)}) copy-start(f32[128,8192]{1,0:T(8,128)} %outer.1) | copy-start | bytes 12582916
  105.9 2.2 %copy-start.2 = (f32[128,8192]{1,0:T(8,128)S(1)}, f32[128,8192]{1,0:T(8,128)}, u32[]{:S(2)}) copy-start(f32[128,8192]{1,0:T(8,128)} %momentum.1) | copy-start | bytes 12582916
  108.1 1.6 %copy-start.3 = (bf16[1,128,8192]{2,1,0:T(8,128)(2,1)S(1)}, bf16[1,128,8192]{2,1,0:T(8,128)(2,1)}, u32[]{:S(2)}) copy-start(bf16[1,128,8192]{2,1,0:T(8,128)(2,1)} %param.22) | copy-start | bytes 6291460
  109.7 5.9 %copy-start.4 = (bf16[1,1,1024,1024]{3,2,1,0:T(8,128)(2,1)S(1)}, bf16[1,1,1024,1024]{3,2,1,0:T(8,128)(2,1)}, u32[]{:S(2)}) copy-start(bf16[1,1,1024,1024]{3,2,1,0:T(8,128)(2,1)} %param.15) | copy-start | bytes 6291460
  109.7 5.9 %copy-start.5 = (bf16[1,1,1024,1024]{3,2,1,0:T(8,128)(2,1)S(1)}, bf16[1,1,1024,1024]{3,2,1,0:T(8,128)(2,1)}, u32[]{:S(2)}) copy-start(bf16[1,1,1024,1024]{3,2,1,0:T(8,128)(2,1)} %param.16) | copy-start | bytes 6291460
  109.7 5.9 %copy-start.6 = (bf16[2,128,1024]{2,1,0:T(8,128)(2,1)S(1)}, bf16[2,128,1024]{2,1,0:T(8,128)(2,1)}, u32[]{:S(2)}) copy-start(bf16[2,128,1024]{2,1,0:T(8,128)(2,1)} %get-tuple-element.20.refs_0_) | copy-start | bytes 1572868
  115.6 1.6 %copy-start.7 = (bf16[1,1,1024,1024]{3,2,1,0:T(8,128)(2,1)S(1)}, bf16[1,1,1024,1024]{3,2,1,0:T(8,128)(2,1)}, u32[]{:S(2)}) copy-start(bf16[1,1,1024,1024]{3,2,1,0:T(8,128)(2,1)} %param.17) | copy-start | bytes 6291460
  115.6 2.2 %copy-start.8 = (bf16[1,1,1024,1024]{3,2,1,0:T(8,128)(2,1)S(1)}, bf16[1,1,1024,1024]{3,2,1,0:T(8,128)(2,1)}, u32[]{:S(2)}) copy-start(bf16[1,1,1024,1024]{3,2,1,0:T(8,128)(2,1)} %param.18) | copy-start | bytes 6291460

commit v4 on v3

--- a/solution.py
+++ b/solution.py
@@ -50,7 +50,7 @@
         functools.partial(gather_kernel, n, width, out_grads.shape[1] // width, order),
         out_shape=[jax.ShapeDtypeStruct((2, rows, width), tokens.dtype)] * n,
         in_specs=[pl.BlockSpec(memory_space=pltpu.SMEM), hbm_spec(), hbm_spec()],
-        out_specs=[any_spec()] * n,
+        out_specs=[vmem_spec()] * n,
         scratch_shapes=[pltpu.SemaphoreType.DMA((2, n))],
         compiler_params=pltpu.CompilerParams(vmem_limit_bytes=60 * MIB),
         cost_estimate=pl.CostEstimate(flops=0, bytes_accessed=16 * n * rows * width, transcendentals=0),
@@ -59,8 +59,17 @@
 
 
 def sum_kernel(
-    chips, own, out, sib, part, inbox, s1, r1, s2, r2, s3, r3, s4, r4
+    chips, own, outer, momentum, local, out, outer_here, momentum_here, local_here,
+    sib, part, inbox, s1, r1, s2, r2, s3, r3, s4, r4, sems,
 ):
+    loads = [
+        pltpu.make_async_copy(src, dst, sems.at[k])
+        for k, (src, dst) in enumerate(
+            ((outer, outer_here), (momentum, momentum_here), (local, local_here))
+        )
+    ]
+    for copy in loads:
+        copy.start()
     me = lax.axis_index("replica")
     chip, core = me // CORES, lax.rem(me, CORES)
     half, wide = own.shape[0] // CORES, own.shape[1] // chips
@@ -131,25 +140,31 @@
         if k:
             second[k].wait_send()
             third[k].wait_send()
-
-
-def replica_sum(snap, replicas):
+    for copy in loads:
+        copy.wait()
+
+
+def replica_sum(snap, outer, momentum, local, replicas):
     chips = replicas // CORES
     rows, cols = snap.shape
     piece = (chips, rows // CORES, cols // chips)
     dma = pltpu.SemaphoreType.DMA((chips,))
     return pl.pallas_call(
         functools.partial(sum_kernel, chips),
-        out_shape=jax.ShapeDtypeStruct(snap.shape, snap.dtype),
-        in_specs=[vmem_spec()],
-        out_specs=vmem_spec(),
-        scratch_shapes=[pltpu.VMEM(piece, snap.dtype)] * 3 + [dma] * 8,
+        out_shape=[
+            jax.ShapeDtypeStruct(x.shape, x.dtype) for x in (snap, outer, momentum, local)
+        ],
+        in_specs=[vmem_spec()] + [hbm_spec()] * 3,
+        out_specs=[vmem_spec()] * 4,
+        scratch_shapes=[pltpu.VMEM(piece, snap.dtype)] * 3
+        + [dma] * 8
+        + [pltpu.SemaphoreType.DMA((3,))],
         compiler_params=pltpu.CompilerParams(
-            collective_id=0, has_side_effects=True, vmem_limit_bytes=16 * MIB
+            collective_id=0, has_side_effects=True, vmem_limit_bytes=36 * MIB
         ),
         cost_estimate=pl.CostEstimate(flops=0, bytes_accessed=100 * snap.size, transcendentals=0),
         name="replica_sum",
-    )(snap)
+    )(snap, outer, momentum, local)
 
 
 def fragment_kernel(
@@ -341,9 +356,11 @@
     for k in range(1, n):
         pairs = [(i, (i + order[k]) % n) for i in range(n)]
         parts.append(lax.ppermute(sent[k], "fsdp", pairs))
-    total = replica_sum(snapshot[0], replicas)
+    total, outer, momentum, local = replica_sum(
+        snapshot[0], outer_params, outer_momentum, local_params[0], replicas
+    )
     outer_next, momentum_next, local_next = fragment(
-        total, outer_params, outer_momentum, snapshot[0], local_params[0], due_rows, replicas
+        total, outer, momentum, snapshot[0], local, due_rows, replicas
     )
     xlt, dr = early(parts[: n // 2], left, right)
     update, first_next, second_next = finish(

time: 128 us -> 64.2 us (0.50)
  Pallas kernels: 114 us -> 52.6 us
  local copies, waits for them, and re-layouts: 4.82 us -> 2.64 us
    pallas_call x1, Pallas kernels: 65.5 us -> 3.71 us  [gather(): pl.pallas_call(functools.partial(gather_kernel, n, width, out_grads.shape...]
    unnamed x20 -> x16, local copies, waits for them, and re-layouts: 4.71 us -> 2.53 us
  transfers between devices with their start and end apart: 3 -> 3, of which waited for: 0 -> 0; matrix products, arithmetic and copies ran while one was open for 0% -> 0% of each run, Pallas kernels for 30% -> 61%
where the time goes in v4:
time: 64.2 us; the launch traced here: 63.9 us
  Pallas kernels  52.6 us (82%)
  starting transfers between devices  7.93 us (12%)
  local copies, waits for them, and re-layouts  2.64 us (4%)
  between operations  0.78 us (1%)
    pallas_call x1, Pallas kernels, replica_sum(): pl.pallas_call(functools.partial(sum_kernel, chips), out_shape=[jax.Shape...  31.8 us
    pallas_call x1, Pallas kernels, finish(): pl.pallas_call(functools.partial(tail_kernel, step, m), out_shape=[jax.Sh...  9.94 us
    ppermute x3, starting transfers between devices, per_device(): parts.append(lax.ppermute(sent[k], 'fsdp', pairs))  7.93 us
    pallas_call x1, Pallas kernels, fragment(): pl.pallas_call(functools.partial(fragment_kernel, step, 1.0 / replicas),...  5.88 us
    pallas_call x1, Pallas kernels, gather(): pl.pallas_call(functools.partial(gather_kernel, n, width, out_grads.shape...  3.71 us
    unnamed x16, local copies, waits for them, and re-layouts  2.53 us
  transfers between devices with their start and end apart: 3, of which 0 were waited for; matrix products, arithmetic and copies ran while one was open for 0% of the time, Pallas kernels for 61%

profile of v4, /device:TPU:0, one launch (start us, length us, event | category | flops | bytes accessed | tf_op | source)
XLA Modules:
  0.0 63.9 jit_solution(3239128934359609954)
XLA Ops:
  0.6 0.0 copy-start.7
  0.6 0.0 copy-start
  0.7 3.7 %gather_slots.1 = (bf16[2,128,1024]{2,1,0:T(8,128)(2,1)}, bf16[2,128,1024]{2,1,0:T(8,128)(2,1)}, bf16[2,128,1024]{2,1,0:T(8,128)(2,1)}, bf16[2,128,1024]{2,1,0:T(8,128)(2,1)}) custom-call(s32[4]{0:T(128)} %ids.1, bf16[128,4096]{1,0:T(8,128)(2,1)} %tokens.1, bf16[128,14336]{1,0:T(8,128)(2,1)} %out_grads.1), custom_call_target="tpu_custom_call" | custom-call | bytes 8388608 | tf_op jit(solution)/shard_map/gather_slots/pallas_call | solution.py:49
  4.4 4.1 %collective-permute-start.2 = (bf16[2,128,1024]{2,1,0:T(8,128)(2,1)}, bf16[2,128,1024]{2,1,0:T(8,128)(2,1)S(1)}, u32[]{:S(2)}, u32[]{:S(2)}) collective-permute-start(bf16[2,128,1024]{2,1,0:T(8,128)(2,1)} %get-tuple-element.25), channel_id=1, source_target_pairs={{0,2},{1,3},{2,0},{3,1},{4,6},{5,7},{6,4},{7,5},{8,10},{9,11},{10,... | collective-permute-start | bytes 1572872 | tf_op jit(solution)/shard_map/ppermute | solution.py:358
  8.5 1.6 %collective-permute-start = (bf16[2,128,1024]{2,1,0:T(8,128)(2,1)}, bf16[2,128,1024]{2,1,0:T(8,128)(2,1)S(1)}, u32[]{:S(2)}, u32[]{:S(2)}) collective-permute-start(bf16[2,128,1024]{2,1,0:T(8,128)(2,1)} %get-tuple-element.22), channel_id=1, source_target_pairs={{0,1},{1,2},{2,3},{3,0},{4,5},{5,6},{6,7},{7,4},{8,9},{9,10},{10,1... | collective-permute-start | bytes 1572872 | tf_op jit(solution)/shard_map/ppermute | solution.py:358
  10.0 2.2 %collective-permute-start.1 = (bf16[2,128,1024]{2,1,0:T(8,128)(2,1)}, bf16[2,128,1024]{2,1,0:T(8,128)(2,1)}, u32[]{:S(2)}, u32[]{:S(2)}) collective-permute-start(bf16[2,128,1024]{2,1,0:T(8,128)(2,1)} %get-tuple-element.23), channel_id=1, source_target_pairs={{0,3},{1,0},{2,1},{3,2},{4,7},{5,4},{6,5},{7,6},{8,11},{9,8},{10,9... | collective-permute-start | bytes 1572872 | tf_op jit(solution)/shard_map/ppermute | solution.py:358
  12.3 0.0 copy-done.7
  12.3 0.1 copy.18.due
  12.4 0.0 copy-done
  12.4 0.0 copy-start.3
  12.4 1.6 %copy-done.3 = bf16[1,128,8192]{2,1,0:T(8,128)(2,1)S(1)} copy-done((bf16[1,128,8192]{2,1,0:T(8,128)(2,1)S(1)}, bf16[1,128,8192]{2,1,0:T(8,128)(2,1)}, u32[]{:S(2)}) %copy-start.3) | copy-done | bytes 2097176
  14.0 31.8 %replica_sum.1 = (bf16[128,8192]{1,0:T(8,128)(2,1)S(1)}, f32[128,8192]{1,0:T(8,128)S(1)}, f32[128,8192]{1,0:T(8,128)S(1)}, bf16[128,8192]{1,0:T(8,128)(2,1)S(1)}) custom-call(bf16[128,8192]{1,0:T(8,128)(2,1)S(1)} %bitcast.11, f32[128,8192]{1,0:T(8,128)} %outer.1, f32[128,8192]{1,0:T(8,128)} %momentum.1, bf16[128,8192]{1,0:T(8,128)(2,1)S(1)} %bitcast.17), custom_call_target="tpu_custom_call" | custom-call | bytes 104857600 | tf_op jit(solution)/shard_map/replica_sum/pallas_call | solution.py:152
  45.8 0.0 copy-start.1
  45.8 0.0 copy-start.2
  45.8 0.0 copy-start.4
  45.8 5.9 %fragment_step.1 = (f32[128,8192]{1,0:T(8,128)}, f32[128,8192]{1,0:T(8,128)}, bf16[128,8192]{1,0:T(8,128)(2,1)}) custom-call(bf16[128,8192]{1,0:T(8,128)(2,1)S(1)} %get-tuple-element.31.total, f32[128,8192]{1,0:T(8,128)S(1)} %get-tuple-element.32.outer, f32[128,8192]{1,0:T(8,128)S(1)} %get-tuple-element.33.momentum, bf16[128,8192]{1,0:T(8,128)(2,1)S(1)} %bitcast.12, ...), custom_call_target="tpu_custom_call" | custom-call | flops 12582912 | bytes 16777216 | tf_op jit(solution)/shard_map/fragment_step/pallas_call | solution.py:199
  51.7 0.0 collective-permute-done.2.refs_1_
  51.7 0.0 copy-done.1
  51.8 0.0 copy-done.2
  51.8 0.0 copy-done.4
  51.8 0.0 copy-start.5
  51.8 0.0 copy-start.6
  51.8 1.3 %early_products.1 = (bf16[1024,256]{1,0:T(8,128)(2,1)S(1)}, bf16[256,1024]{1,0:T(8,128)(2,1)S(1)}) custom-call(bf16[2,128,1024]{2,1,0:T(8,128)(2,1)S(1)} %copy-done.4, bf16[2,128,1024]{2,1,0:T(8,128)(2,1)S(1)} %collective-permute-done.2.refs_1_, bf16[1024,1024]{1,0:T(8,128)(2,1)S(1)} %bitcast.13, bf16[1024,1024]{1,0:T(8,128)(2,1)S(1)} %bitcast.15), custom_call_target="tpu_custom_call" | custom-call | flops 1073741824 | bytes 8388608 | tf_op jit(solution)/shard_map/early_products/pallas_call | solution.py:237
  53.1 0.0 collective-permute-done.refs_0_
  53.1 0.0 collective-permute-done.1.refs_1_
  53.1 0.3 copy-done.5
  53.4 0.6 copy-done.6
  54.0 9.9 %soap_tail.1 = (bf16[1024,1024]{1,0:T(8,128)(2,1)}, bf16[1024,1024]{1,0:T(8,128)(2,1)}, bf16[1024,1024]{1,0:T(8,128)(2,1)}) custom-call(bf16[2,128,1024]{2,1,0:T(8,128)(2,1)S(1)} %collective-permute-done.refs_0_, bf16[2,128,1024]{2,1,0:T(8,128)(2,1)} %collective-permute-done.1.refs_1_, bf16[1024,256]{1,0:T(8,128)(2,1)S(1)} %get-tuple-element.26.refs_2_, ...), custom_call_target="tpu_custom_call" | custom-call | flops 6442450944 | bytes 14680064 | tf_op jit(solution)/shard_map/soap_tail/pallas_call | solution.py:317
Async XLA Ops:
  0.6 11.7 %copy-start.7 = (s32[128]{0:T(128)S(1)}, s32[128]{0:T(128)}, u32[]{:S(2)}) copy-start(s32[128]{0:T(128)} %param.23) | copy-start | bytes 1540
  0.6 11.8 %copy-start = (bf16[1,128,8192]{2,1,0:T(8,128)(2,1)S(1)}, bf16[1,128,8192]{2,1,0:T(8,128)(2,1)}, u32[]{:S(2)}) copy-start(bf16[1,128,8192]{2,1,0:T(8,128)(2,1)} %param.21) | copy-start | bytes 6291460
  4.4 47.4 %collective-permute-start.2 = (bf16[2,128,1024]{2,1,0:T(8,128)(2,1)}, bf16[2,128,1024]{2,1,0:T(8,128)(2,1)S(1)}, u32[]{:S(2)}, u32[]{:S(2)}) collective-permute-start(bf16[2,128,1024]{2,1,0:T(8,128)(2,1)} %get-tuple-element.25), channel_id=1, source_target_pairs={{0,2},{1,3},{2,0},{3,1},{4,6},{5,7},{6,4},{7,5},{8,10},{9,11},{10,... | collective-permute-start | bytes 1572872 | tf_op jit(solution)/shard_map/ppermute | solution.py:358
  8.5 44.6 %collective-permute-start = (bf16[2,128,1024]{2,1,0:T(8,128)(2,1)}, bf16[2,128,1024]{2,1,0:T(8,128)(2,1)S(1)}, u32[]{:S(2)}, u32[]{:S(2)}) collective-permute-start(bf16[2,128,1024]{2,1,0:T(8,128)(2,1)} %get-tuple-element.22), channel_id=1, source_target_pairs={{0,1},{1,2},{2,3},{3,0},{4,5},{5,6},{6,7},{7,4},{8,9},{9,10},{10,1... | collective-permute-start | bytes 1572872 | tf_op jit(solution)/shard_map/ppermute | solution.py:358
  10.0 43.0 %collective-permute-start.1 = (bf16[2,128,1024]{2,1,0:T(8,128)(2,1)}, bf16[2,128,1024]{2,1,0:T(8,128)(2,1)}, u32[]{:S(2)}, u32[]{:S(2)}) collective-permute-start(bf16[2,128,1024]{2,1,0:T(8,128)(2,1)} %get-tuple-element.23), channel_id=1, source_target_pairs={{0,3},{1,0},{2,1},{3,2},{4,7},{5,4},{6,5},{7,6},{8,11},{9,8},{10,9... | collective-permute-start | bytes 1572872 | tf_op jit(solution)/shard_map/ppermute | solution.py:358
  12.4 1.6 %copy-start.3 = (bf16[1,128,8192]{2,1,0:T(8,128)(2,1)S(1)}, bf16[1,128,8192]{2,1,0:T(8,128)(2,1)}, u32[]{:S(2)}) copy-start(bf16[1,128,8192]{2,1,0:T(8,128)(2,1)} %param.22) | copy-start | bytes 6291460
  45.8 5.9 %copy-start.1 = (bf16[1,1,1024,1024]{3,2,1,0:T(8,128)(2,1)S(1)}, bf16[1,1,1024,1024]{3,2,1,0:T(8,128)(2,1)}, u32[]{:S(2)}) copy-start(bf16[1,1,1024,1024]{3,2,1,0:T(8,128)(2,1)} %param.15) | copy-start | bytes 6291460
  45.8 5.9 %copy-start.2 = (bf16[1,1,1024,1024]{3,2,1,0:T(8,128)(2,1)S(1)}, bf16[1,1,1024,1024]{3,2,1,0:T(8,128)(2,1)}, u32[]{:S(2)}) copy-start(bf16[1,1,1024,1024]{3,2,1,0:T(8,128)(2,1)} %param.16) | copy-start | bytes 6291460
  45.8 5.9 %copy-start.4 = (bf16[2,128,1024]{2,1,0:T(8,128)(2,1)S(1)}, bf16[2,128,1024]{2,1,0:T(8,128)(2,1)}, u32[]{:S(2)}) copy-start(bf16[2,128,1024]{2,1,0:T(8,128)(2,1)} %get-tuple-element.24.refs_0_) | copy-start | bytes 1572868
  51.8 1.6 %copy-start.5 = (bf16[1,1,1024,1024]{3,2,1,0:T(8,128)(2,1)S(1)}, bf16[1,1,1024,1024]{3,2,1,0:T(8,128)(2,1)}, u32[]{:S(2)}) copy-start(bf16[1,1,1024,1024]{3,2,1,0:T(8,128)(2,1)} %param.17) | copy-start | bytes 6291460
  51.8 2.2 %copy-start.6 = (bf16[1,1,1024,1024]{3,2,1,0:T(8,128)(2,1)S(1)}, bf16[1,1,1024,1024]{3,2,1,0:T(8,128)(2,1)}, u32[]{:S(2)}) copy-start(bf16[1,1,1024,1024]{3,2,1,0:T(8,128)(2,1)} %param.18) | copy-start | bytes 6291460
